TPU v7x, 128 devices: a whole 4x4x4 slice. The times are simulated.
128 devices in a mesh: dp: 4 (over x), expert: 32 (over z, y, core).
Axes of the slice: x: 4, y: 4, z: 4, core: 2. Of those that a mesh axis runs over, the one named last changes fastest.
Arguments:
- tokens: bfloat16 [32768, 1536], P(('dp', 'expert')), may hold values from -6 to 6
- routes: int32 [32768, 4], P(('dp', 'expert')), may hold values from 0 to 31, all different within a row; in each aligned block of 256 rows (0 to 255, 256 to 511, ...) at most 40 rows name the same one
- w_query: bfloat16 [1536, 1536], P('dp'), may hold values from -0.15625 to 0.15625
- key_matrix: bfloat16 [1536, 256], P('dp'), may hold values from -0.15625 to 0.15625
- value_matrix: bfloat16 [1536, 256], P('dp'), may hold values from -0.15625 to 0.15625
- w_output: bfloat16 [1536, 1536], P('dp'), may hold values from -0.625 to 0.625
- norm_one: bfloat16 [1536], P('dp'), may hold values from 0.5 to 1.5
- norm_two: bfloat16 [1536], P('dp'), may hold values from 0.5 to 1.5
- w_router: bfloat16 [1536, 32], P('dp'), may hold values from -0.078125 to 0.078125
- w_gate: bfloat16 [32, 1536, 768], P('expert', 'dp'), may hold values from -0.15625 to 0.15625
- w_up: bfloat16 [32, 1536, 768], P('expert', 'dp'), may hold values from -0.15625 to 0.15625
- w_down: bfloat16 [32, 1536, 768], P('expert', 'dp'), may hold values from -0.4375 to 0.4375
- cotangent: bfloat16 [32768, 1536], P(('dp', 'expert')), may hold values from -6 to 6
Outputs:
- mixed: bfloat16 [32768, 1536], P(('dp', 'expert'))
- grad_tokens: float32 [32768, 1536], P(('dp', 'expert'))
- grad_query: float32 [1536, 1536], P('dp')
- grad_key: float32 [1536, 256], P('dp')
- grad_value: float32 [1536, 256], P('dp')
- grad_output: float32 [1536, 1536], P('dp')
- grad_norm_one: float32 [1536], P('dp')
- grad_norm_two: float32 [1536], P('dp')
- grad_router: float32 [1536, 32], P('dp')
- grad_gate: float32 [32, 1536, 768], P('expert', 'dp')
- grad_up: float32 [32, 1536, 768], P('expert', 'dp')
- grad_down: float32 [32, 1536, 768], P('expert', 'dp')
Inputs may be any that keep to these rules, and one draw needn't show every extreme that they name: `routes`: each row names 4 different experts. In each aligned block of 256 rows (one sequence) no expert is named by more than 40 rows, and in every draw some block names some expert exactly 40 times.
All inputs are finite; a program needn't handle non-finite values.
Results may differ from a plain program's by a relative error of at most 0.025.
Values may be sent and summed in bfloat16 or wider, within the bound.
A program may use at most 192 MiB of HBM per device.

v0:
```python
import jax
import jax.numpy as jnp
from jax import lax
from jax.sharding import PartitionSpec as P

MODEL_WIDTH = 1536
QUERY_HEADS = 12
KEY_VALUE_HEADS = 2
HEAD_SIZE = 128
TOPK = 4


EPSILON = 1e-06
ROPE_BASE = 10000.0


def scaled_norm(values, gain_vector):
    return (
        values
        * lax.rsqrt(jnp.mean(values * values, axis=-1, keepdims=True) + EPSILON)
        * gain_vector
    )


def apply_rotary(values, head_count):
    sequence_length = values.shape[0]
    shaped = values.reshape(sequence_length, head_count, HEAD_SIZE)
    half_dim = HEAD_SIZE // 2
    position = jnp.arange(sequence_length).astype(jnp.float32)
    frequency = ROPE_BASE ** (-jnp.arange(half_dim).astype(jnp.float32) * 2.0 / HEAD_SIZE)
    angles = position[:, None] * frequency[None, :]
    cosine = jnp.cos(angles)[:, None, :]
    sine_part = jnp.sin(angles)[:, None, :]
    first_half = shaped[..., :half_dim]
    second_half = shaped[..., half_dim:]
    turned = jnp.concatenate(
        [
            first_half * cosine - second_half * sine_part,
            second_half * cosine + first_half * sine_part,
        ],
        axis=-1,
    )
    return turned.reshape(sequence_length, head_count * HEAD_SIZE)


def gelu_tanh(values):
    return (
        0.5
        * values
        * (1.0 + jnp.tanh(0.7978845608028654 * (values + 0.044715 * values * values * values)))
    )


def gated_unit(gate_values, up_values):
    return gelu_tanh(gate_values) * up_values


def contract(left_side, right_side, left_dim, right_dim):
    return lax.dot_general(
        left_side,
        right_side,
        (((left_dim,), (right_dim,)), ((), ())),
        preferred_element_type=jnp.float32,
    )


def slot_tables(route_rows, experts, capacity):
    assigned = route_rows.reshape(-1)
    onehot = (assigned[:, None] == jnp.arange(experts, dtype=jnp.int32)[None, :]).astype(jnp.int32)
    before = jnp.cumsum(onehot, axis=0) - onehot
    within = jnp.sum(before * onehot, axis=1)
    target = assigned * capacity + within
    count_all = assigned.shape[0]
    owners = (
        jnp.zeros((experts * capacity,), jnp.int32)
        .at[target]
        .set(jnp.arange(count_all, dtype=jnp.int32))
    )
    filled = jnp.zeros((experts * capacity,), jnp.int32).at[target].set(1)
    return (target, owners, filled)


def by_expert(received, local_experts):
    item_count = received.shape[1]
    grouped = received.reshape(-1, local_experts, item_count, MODEL_WIDTH)
    return jnp.transpose(grouped, (1, 0, 2, 3)).reshape(local_experts, -1, MODEL_WIDTH)


def by_source(produced, local_experts, item_count):
    grouped = produced.reshape(local_experts, -1, item_count, MODEL_WIDTH)
    return jnp.transpose(grouped, (1, 0, 2, 3)).reshape(-1, item_count, MODEL_WIDTH)


def shards(
    tokens,
    routes,
    w_query,
    key_matrix,
    value_matrix,
    w_output,
    norm_one,
    norm_two,
    w_router,
    w_gate,
    w_up,
    w_down,
    cotangent,
):
    sequence_length = tokens.shape[0]
    head_groups = QUERY_HEADS // KEY_VALUE_HEADS
    experts = w_router.shape[1]
    capacity = 5 * sequence_length * TOPK // (4 * experts)
    local_experts = w_gate.shape[0]
    score_scale = HEAD_SIZE ** (-0.5)
    rows_per_block = min(sequence_length, 512)
    count_of_blocks = sequence_length // rows_per_block
    full_query, full_key, full_value, full_output, gain_one, gain_two, full_router = (
        lax.all_gather(w_query, "dp", axis=0, tiled=True),
        lax.all_gather(key_matrix, "dp", axis=0, tiled=True),
        lax.all_gather(value_matrix, "dp", axis=0, tiled=True),
        lax.all_gather(w_output, "dp", axis=0, tiled=True),
        lax.all_gather(norm_one, "dp", axis=0, tiled=True),
        lax.all_gather(norm_two, "dp", axis=0, tiled=True),
        lax.all_gather(w_router, "dp", axis=0, tiled=True),
    )
    gate_full, up_full, down_full = (
        lax.all_gather(w_gate, "dp", axis=1, tiled=True),
        lax.all_gather(w_up, "dp", axis=1, tiled=True),
        lax.all_gather(w_down, "dp", axis=1, tiled=True),
    )
    inputs = tokens.astype(jnp.float32)
    normed_exact, norm_back_one = jax.vjp(scaled_norm, inputs, gain_one.astype(jnp.float32))
    normed = normed_exact.astype(jnp.bfloat16)
    unrotated_query = jnp.dot(normed, full_query, preferred_element_type=jnp.float32)
    unrotated_key = jnp.dot(normed, full_key, preferred_element_type=jnp.float32)
    projected_value = jnp.dot(normed, full_value, preferred_element_type=jnp.float32)
    rotated_query, rotate_query_back = jax.vjp(
        lambda record_entries: apply_rotary(record_entries, QUERY_HEADS), unrotated_query
    )
    rotated_key, unrotate_key_gradient = jax.vjp(
        lambda record_entries: apply_rotary(record_entries, KEY_VALUE_HEADS), unrotated_key
    )
    query_rows = rotated_query.astype(jnp.bfloat16).reshape(
        sequence_length, KEY_VALUE_HEADS, head_groups, HEAD_SIZE
    )
    per_head_keys = rotated_key.astype(jnp.bfloat16).reshape(
        sequence_length, KEY_VALUE_HEADS, HEAD_SIZE
    )
    per_head_values = projected_value.astype(jnp.bfloat16).reshape(
        sequence_length, KEY_VALUE_HEADS, HEAD_SIZE
    )
    blocked_queries = query_rows.reshape(
        count_of_blocks, rows_per_block, KEY_VALUE_HEADS, head_groups, HEAD_SIZE
    )
    block_starts = jnp.arange(count_of_blocks, dtype=jnp.int32) * rows_per_block

    def masked_scores(query_block, first_row):
        scores = (
            jnp.einsum(
                "ihgd,jhd->hgij", query_block, per_head_keys, preferred_element_type=jnp.float32
            )
            * score_scale
        )
        row_index = first_row + jnp.arange(rows_per_block, dtype=jnp.int32)[:, None]
        column_index = jnp.arange(sequence_length, dtype=jnp.int32)[None, :]
        return jnp.where(column_index <= row_index, scores, -jnp.inf)

    def attend(block_pair):
        scores = masked_scores(block_pair[0], block_pair[1])
        largest = jnp.max(scores, axis=-1, keepdims=True)
        exponent = jnp.exp(scores - largest)
        row_total = jnp.sum(exponent, axis=-1, keepdims=True)
        softmax_weights = (exponent / row_total).astype(jnp.bfloat16)
        block_out = jnp.einsum(
            "hgij,jhd->ihgd", softmax_weights, per_head_values, preferred_element_type=jnp.float32
        )
        return (block_out.astype(jnp.bfloat16), largest[..., 0] + jnp.log(row_total[..., 0]))

    mixed_blocks, log_totals = lax.map(attend, (blocked_queries, block_starts))
    mixed_heads = mixed_blocks.reshape(sequence_length, QUERY_HEADS * HEAD_SIZE)
    attended = jnp.dot(mixed_heads, full_output, preferred_element_type=jnp.float32)
    residual = inputs + attended
    second_exact, norm_back_two = jax.vjp(scaled_norm, residual, gain_two.astype(jnp.float32))
    second = second_exact.astype(jnp.bfloat16)
    logits = jnp.dot(tokens, full_router, preferred_element_type=jnp.float32)
    onehot = (routes[:, :, None] == jnp.arange(experts, dtype=jnp.int32)[None, None, :]).astype(
        jnp.float32
    )
    chosen = jnp.sum(onehot * logits[:, None, :], axis=-1)
    chosen_top = jnp.max(chosen, axis=-1, keepdims=True)
    chosen_exp = jnp.exp(chosen - chosen_top)
    gate_share = chosen_exp / jnp.sum(chosen_exp, axis=-1, keepdims=True)
    target, owners, filled = slot_tables(routes, experts, capacity)
    used_slot = (filled > 0)[:, None]
    send_rows = jnp.where(used_slot, second[owners // TOPK], jnp.zeros((), jnp.bfloat16)).reshape(
        experts, capacity, MODEL_WIDTH
    )
    received = lax.all_to_all(send_rows, "expert", split_axis=0, concat_axis=0, tiled=True)
    item_count = received.shape[1]
    grouped = by_expert(received, local_experts)
    gate_pre = jnp.einsum("erd,edf->erf", grouped, gate_full, preferred_element_type=jnp.float32)
    up_pre = jnp.einsum("erd,edf->erf", grouped, up_full, preferred_element_type=jnp.float32)
    hidden = gated_unit(gate_pre, up_pre).astype(jnp.bfloat16)
    produced = jnp.einsum(
        "erf,edf->erd", hidden, down_full, preferred_element_type=jnp.float32
    ).astype(jnp.bfloat16)
    brought_back = lax.all_to_all(
        by_source(produced, local_experts, item_count),
        "expert",
        split_axis=0,
        concat_axis=0,
        tiled=True,
    )
    returned = (
        brought_back.reshape(experts * capacity, MODEL_WIDTH)[target]
        .reshape(sequence_length, TOPK, MODEL_WIDTH)
        .astype(jnp.float32)
    )
    combined = jnp.sum(gate_share[:, :, None] * returned, axis=1)
    output = (residual + combined).astype(jnp.bfloat16)
    upstream = cotangent.astype(jnp.float32)
    gate_grad = jnp.sum(returned * upstream[:, None, :], axis=-1)
    chosen_grad = gate_share * (gate_grad - jnp.sum(gate_share * gate_grad, axis=-1, keepdims=True))
    logit_grad = jnp.sum(onehot * chosen_grad[:, :, None], axis=1).astype(jnp.bfloat16)
    router_grad = contract(tokens, logit_grad, 0, 0)
    input_grad = contract(logit_grad, full_router, 1, 1)
    row_grads = (
        (gate_share[:, :, None] * upstream[:, None, :])
        .astype(jnp.bfloat16)
        .reshape(sequence_length * TOPK, MODEL_WIDTH)
    )
    send_grads = jnp.where(used_slot, row_grads[owners], jnp.zeros((), jnp.bfloat16)).reshape(
        experts, capacity, MODEL_WIDTH
    )
    grads_in = lax.all_to_all(send_grads, "expert", split_axis=0, concat_axis=0, tiled=True)
    grad_grouped = by_expert(grads_in, local_experts)
    input_grouped = by_expert(received, local_experts)
    gate_pre = jnp.einsum(
        "erd,edf->erf", input_grouped, gate_full, preferred_element_type=jnp.float32
    )
    up_pre = jnp.einsum("erd,edf->erf", input_grouped, up_full, preferred_element_type=jnp.float32)
    hidden_exact, gated_back = jax.vjp(gated_unit, gate_pre, up_pre)
    hidden = hidden_exact.astype(jnp.bfloat16)
    down_grad = jnp.einsum("erd,erf->edf", grad_grouped, hidden, preferred_element_type=jnp.float32)
    hidden_grad = jnp.einsum(
        "erd,edf->erf", grad_grouped, down_full, preferred_element_type=jnp.float32
    )
    gate_pre_grad, up_pre_grad = gated_back(hidden_grad)
    gate_pre_grad = gate_pre_grad.astype(jnp.bfloat16)
    up_pre_grad = up_pre_grad.astype(jnp.bfloat16)
    gate_weight_grad = jnp.einsum(
        "erd,erf->edf", input_grouped, gate_pre_grad, preferred_element_type=jnp.float32
    )
    up_weight_grad = jnp.einsum(
        "erd,erf->edf", input_grouped, up_pre_grad, preferred_element_type=jnp.float32
    )
    row_back = jnp.einsum(
        "erf,edf->erd", gate_pre_grad, gate_full, preferred_element_type=jnp.float32
    )
    row_back = (
        row_back
        + jnp.einsum("erf,edf->erd", up_pre_grad, up_full, preferred_element_type=jnp.float32)
    ).astype(jnp.bfloat16)
    returned_grads = lax.all_to_all(
        by_source(row_back, local_experts, capacity),
        "expert",
        split_axis=0,
        concat_axis=0,
        tiled=True,
    )
    second_grad = jnp.sum(
        returned_grads.reshape(experts * capacity, MODEL_WIDTH)[target]
        .reshape(sequence_length, TOPK, MODEL_WIDTH)
        .astype(jnp.float32),
        axis=1,
    )
    expert_shares = (
        lax.psum_scatter(
            gate_weight_grad.astype(jnp.bfloat16), "dp", scatter_dimension=1, tiled=True
        ).astype(jnp.float32),
        lax.psum_scatter(
            up_weight_grad.astype(jnp.bfloat16), "dp", scatter_dimension=1, tiled=True
        ).astype(jnp.float32),
        lax.psum_scatter(
            down_grad.astype(jnp.bfloat16), "dp", scatter_dimension=1, tiled=True
        ).astype(jnp.float32),
    )
    residual_part, gain_two_grad = norm_back_two(second_grad)
    residual_grad = upstream + residual_part
    attended_grad = residual_grad.astype(jnp.bfloat16)
    output_weight_grad = contract(mixed_heads, attended_grad, 0, 0)
    attention_mix_gradient = contract(attended_grad, full_output, 1, 1).astype(jnp.bfloat16)
    blocked_mix_gradient = attention_mix_gradient.reshape(
        count_of_blocks, rows_per_block, KEY_VALUE_HEADS, head_groups, HEAD_SIZE
    )

    def attend_back(running, pieces):
        key_sum, value_sum = running
        query_block, grad_block, log_block, first_row = pieces
        scores = masked_scores(query_block, first_row)
        softmax_exact = jnp.exp(scores - log_block[..., None])
        value_sum = value_sum + jnp.einsum(
            "hgij,ihgd->jhd",
            softmax_exact.astype(jnp.bfloat16),
            grad_block,
            preferred_element_type=jnp.float32,
        )
        weight_grad = jnp.einsum(
            "ihgd,jhd->hgij", grad_block, per_head_values, preferred_element_type=jnp.float32
        )
        row_delta = jnp.sum(softmax_exact * weight_grad, axis=-1, keepdims=True)
        score_grad = (softmax_exact * (weight_grad - row_delta)).astype(jnp.bfloat16)
        query_grad = (
            jnp.einsum(
                "hgij,jhd->ihgd", score_grad, per_head_keys, preferred_element_type=jnp.float32
            )
            * score_scale
        )
        key_sum = (
            key_sum
            + jnp.einsum(
                "hgij,ihgd->jhd", score_grad, query_block, preferred_element_type=jnp.float32
            )
            * score_scale
        )
        return ((key_sum, value_sum), query_grad)

    blank_head_slots = jnp.zeros((sequence_length, KEY_VALUE_HEADS, HEAD_SIZE), jnp.float32)
    (gradient_of_key, gradient_of_value), query_grads = lax.scan(
        attend_back,
        (blank_head_slots, blank_head_slots),
        (blocked_queries, blocked_mix_gradient, log_totals, block_starts),
    )
    query_pre_grad = rotate_query_back(
        query_grads.reshape(sequence_length, QUERY_HEADS * HEAD_SIZE)
    )[0].astype(jnp.bfloat16)
    unrotated_key_gradient = unrotate_key_gradient(
        gradient_of_key.reshape(sequence_length, KEY_VALUE_HEADS * HEAD_SIZE)
    )[0].astype(jnp.bfloat16)
    projected_value_gradient = gradient_of_value.reshape(
        sequence_length, KEY_VALUE_HEADS * HEAD_SIZE
    ).astype(jnp.bfloat16)
    normed_grad = contract(query_pre_grad, full_query, 1, 1)
    normed_grad = (
        normed_grad
        + contract(unrotated_key_gradient, full_key, 1, 1)
        + contract(projected_value_gradient, full_value, 1, 1)
    )
    query_weight_grad = contract(normed, query_pre_grad, 0, 0)
    key_weight_grad = contract(normed, unrotated_key_gradient, 0, 0)
    value_weight_grad = contract(normed, projected_value_gradient, 0, 0)
    input_part, gain_one_grad = norm_back_one(normed_grad)
    input_grad = input_grad + residual_grad + input_part
    layer_grads = (
        query_weight_grad,
        key_weight_grad,
        value_weight_grad,
        output_weight_grad,
        gain_one_grad,
        gain_two_grad,
        router_grad,
    )
    summed = (
        lax.psum(layer_grads[0].astype(jnp.bfloat16), "expert").astype(jnp.float32),
        lax.psum(layer_grads[1].astype(jnp.bfloat16), "expert").astype(jnp.float32),
        lax.psum(layer_grads[2].astype(jnp.bfloat16), "expert").astype(jnp.float32),
        lax.psum(layer_grads[3].astype(jnp.bfloat16), "expert").astype(jnp.float32),
        lax.psum(layer_grads[4].astype(jnp.bfloat16), "expert").astype(jnp.float32),
        lax.psum(layer_grads[5].astype(jnp.bfloat16), "expert").astype(jnp.float32),
        lax.psum(layer_grads[6].astype(jnp.bfloat16), "expert").astype(jnp.float32),
    )
    shares = (
        lax.psum_scatter(
            summed[0].astype(jnp.bfloat16), "dp", scatter_dimension=0, tiled=True
        ).astype(jnp.float32),
        lax.psum_scatter(
            summed[1].astype(jnp.bfloat16), "dp", scatter_dimension=0, tiled=True
        ).astype(jnp.float32),
        lax.psum_scatter(
            summed[2].astype(jnp.bfloat16), "dp", scatter_dimension=0, tiled=True
        ).astype(jnp.float32),
        lax.psum_scatter(
            summed[3].astype(jnp.bfloat16), "dp", scatter_dimension=0, tiled=True
        ).astype(jnp.float32),
        lax.psum_scatter(
            summed[4].astype(jnp.bfloat16), "dp", scatter_dimension=0, tiled=True
        ).astype(jnp.float32),
        lax.psum_scatter(
            summed[5].astype(jnp.bfloat16), "dp", scatter_dimension=0, tiled=True
        ).astype(jnp.float32),
        lax.psum_scatter(
            summed[6].astype(jnp.bfloat16), "dp", scatter_dimension=0, tiled=True
        ).astype(jnp.float32),
    )
    return (
        output,
        input_grad,
        shares[0],
        shares[1],
        shares[2],
        shares[3],
        shares[4],
        shares[5],
        shares[6],
        expert_shares[0],
        expert_shares[1],
        expert_shares[2],
    )


def solution(mesh):
    placed = (
        P(("dp", "expert"), None),
        P(("dp", "expert"), None),
        P("dp", None),
        P("dp", None),
        P("dp", None),
        P("dp", None),
        P("dp"),
        P("dp"),
        P("dp", None),
        P("expert", "dp", None),
        P("expert", "dp", None),
        P("expert", "dp", None),
        P(("dp", "expert"), None),
    )
    return jax.shard_map(
        shards,
        mesh=mesh,
        in_specs=placed,
        out_specs=(
            P(("dp", "expert"), None),
            P(("dp", "expert"), None),
            P("dp", None),
            P("dp", None),
            P("dp", None),
            P("dp", None),
            P("dp"),
            P("dp"),
            P("dp", None),
            P("expert", "dp", None),
            P("expert", "dp", None),
            P("expert", "dp", None),
        ),
        check_vma=False,
    )
```

profile of v0, /device:TPU:1, one launch (start us, length us, event | category | flops | bytes accessed | tf_op | source)
XLA Modules:
  0.0 858.1 jit_solution(1335807985613341386)
XLA Ops:
  10.8 9.3 %all-gather.1 = bf16[4,1,384]{2,1,0:T(2,128)(2,1)S(1)} all-gather(bf16[1,1,384]{2,1,0:T(2,128)(2,1)S(1)} %reshape.494), channel_id=1, replica_groups=mesh['dp'=4,'expert'=32] {'dp'}, dimensions={0}, use_global_device_ids=true | all-gather | bytes 3840 | tf_op jit(solution)/shard_map/all_gather | solution.py:123
  20.1 8.4 all-gather
  28.6 10.8 %all_gather.35 = bf16[1536,32]{0,1:T(8,128)(2,1)S(1)} all-gather(bf16[384,32]{0,1:T(8,128)(2,1)S(1)} %copy-done.55), channel_id=1, replica_groups=mesh['dp'=4,'expert'=32] {'dp'}, dimensions={0}, use_global_device_ids=true | all-gather | bytes 122880 | tf_op jit(solution)/shard_map/all_gather | solution.py:124
  43.1 9.0 %reduce-window.6 = s32[32,8,128]{2,1,0:T(8,128)S(1)} reduce-window(s32[32,8,128]{2,1,0:T(8,128)S(1)} %fusion.52, s32[]{:T(128)} %constant.59.clone.1), window={size=1x1x128 pad=0_0x0_0x127_0}, to_apply=%region_6.7 | reduce-window | flops 4161536 | bytes 262148 | tf_op jit(solution)/shard_map/reduce-window
  52.6 4.3 scatter_custom_fusion.1
  57.0 4.3 scatter_custom_fusion
  62.0 10.6 %all_gather.32 = bf16[1536,256]{1,0:T(8,128)(2,1)S(1)} all-gather(bf16[384,256]{1,0:T(8,128)(2,1)S(1)} %copy-done.39), channel_id=1, replica_groups=mesh['dp'=4,'expert'=32] {'dp'}, dimensions={0}, use_global_device_ids=true | all-gather | bytes 983040 | tf_op jit(solution)/shard_map/all_gather | solution.py:119
  75.8 14.4 %all_gather.31 = bf16[1536,256]{1,0:T(8,128)(2,1)S(1)} all-gather(bf16[384,256]{1,0:T(8,128)(2,1)S(1)} %copy-done.40), channel_id=1, replica_groups=mesh['dp'=4,'expert'=32] {'dp'}, dimensions={0}, use_global_device_ids=true | all-gather | bytes 983040 | tf_op jit(solution)/shard_map/all_gather | solution.py:120
  95.8 7.8 mul.600
  107.5 5.6 gather_fusion.2
  114.3 4.8 fusion.70
  126.3 3.8 multiply_reduce_fusion.4
  130.9 5.5 gather_fusion
  136.4 6.0 broadcast_select_fusion
  142.3 19.8 %all-to-all-start = ((bf16[32,40,1536]{2,1,0:T(8,128)(2,1)}), bf16[32,40,1536]{2,1,0:T(8,128)(2,1)}, u32[]{:S(2)}, u32[]{:S(2)}) async-start(bf16[32,40,1536]{2,1,0:T(8,128)(2,1)} %get-tuple-element.90), calls=%async_computation | async-start | bytes 7864320 | tf_op jit(solution)/shard_map/all_to_all | solution.py:198
  162.7 47.0 %all-to-all-done = bf16[32,40,1536]{2,1,0:T(8,128)(2,1)} async-done(((bf16[32,40,1536]{2,1,0:T(8,128)(2,1)}), bf16[32,40,1536]{2,1,0:T(8,128)(2,1)}, u32[]{:S(2)}, u32[]{:S(2)}) %all-to-all-start) | async-done | bytes 3932192 | tf_op jit(solution)/shard_map/all_to_all | solution.py:198
  209.7 7.8 all-to-all-start.2
  218.1 8.0 fusion.20
  226.1 8.2 fusion.24
  234.2 18.0 %all-gather.16.cloned.1.call-done = bf16[1,1536,768]{2,1,0:T(8,128)(2,1)} async-done(((bf16[1,384,768]{2,1,0:T(8,128)(2,1)}), bf16[1,1536,768]{2,1,0:T(8,128)(2,1)}) %all-gather.16.cloned.1.call-update) | async-done | bytes 2359312 | tf_op jit(solution)/shard_map/all_gather | solution.py:129
  252.3 12.9 %all-to-all-done.2 = bf16[32,40,1536]{2,1,0:T(8,128)(2,1)} async-done(((bf16[32,40,1536]{2,1,0:T(8,128)(2,1)}), bf16[32,40,1536]{2,1,0:T(8,128)(2,1)}, u32[]{:S(2)}, u32[]{:S(2)}) %all-to-all-start.2) | async-done | bytes 3932192 | tf_op jit(solution)/shard_map/all_to_all | solution.py:235
  265.2 12.0 %multiply_convert_fusion.1 = (bf16[1280,768]{1,0:T(8,128)(2,1)}, bf16[1280,768]{1,0:T(8,128)(2,1)}, bf16[1280,768]{1,0:T(8,128)(2,1)S(1)}) fusion(f32[1280,768]{1,0:T(8,128)} %fusion.24, f32[1280,768]{1,0:T(8,128)} %fusion.20, bf16[1280,1536]{1,0:T(8,128)(2,1)} %bitcast.23, bf16[1,1536,768]{2,1,0:T(8,128)(2,1)} %all-gather.16.cloned.1.call-done), kind=kOutput, calls=%fused_computation.24 | convolution fusion | flops 3049390080 | bytes 20054016 | tf_op jit(solution)/shard_map/erd,edf->erf/dot_general | solution.py:245
  277.2 4.9 convolution_convert_fusion.2
  282.0 8.1 all-to-all-start.1
  290.2 5.7 fusion.22
  295.8 4.9 fusion
  300.8 36.8 %all-to-all-done.1 = bf16[32,40,1536]{2,1,0:T(8,128)(2,1)} async-done(((bf16[32,40,1536]{2,1,0:T(8,128)(2,1)}), bf16[32,40,1536]{2,1,0:T(8,128)(2,1)}, u32[]{:S(2)}, u32[]{:S(2)}) %all-to-all-start.1) | async-done | bytes 3932192 | tf_op jit(solution)/shard_map/all_to_all | solution.py:207
  337.6 7.9 all-to-all-start.3
  347.6 9.9 %gather_fusion.1 = bf16[1024,1536]{1,0:T(8,128)(2,1)} fusion(bf16[1280,1536]{1,0:T(8,128)(2,1)} %bitcast.21, s32[1024]{0:T(1024)S(1)} %broadcast_clamp_fusion), kind=kCustom, calls=%fused_computation.1 | custom fusion | bytes 6295552 | tf_op jit(solution)/shard_map/gather | solution.py:215
  357.5 6.7 reshape.440
  364.2 29.0 %all-to-all-done.3 = bf16[32,40,1536]{2,1,0:T(8,128)(2,1)} async-done(((bf16[32,40,1536]{2,1,0:T(8,128)(2,1)}), bf16[32,40,1536]{2,1,0:T(8,128)(2,1)}, u32[]{:S(2)}, u32[]{:S(2)}) %all-to-all-start.3) | async-done | bytes 3932192 | tf_op jit(solution)/shard_map/all_to_all | solution.py:264
  393.2 9.9 %gather_fusion.3 = bf16[1024,1536]{1,0:T(8,128)(2,1)} fusion(bf16[1280,1536]{1,0:T(8,128)(2,1)} %bitcast.25, s32[1024]{0:T(1024)S(1)} %broadcast_clamp_fusion), kind=kCustom, calls=%fused_computation.3 | custom fusion | bytes 6295552 | tf_op jit(solution)/shard_map/gather | solution.py:272
  403.1 6.7 reshape.441
  409.7 7.7 reduce_sum.175
  419.9 18.7 %multiply_reduce_fusion = (f32[256,4]{1,0:T(8,128)}, f32[256,1536]{1,0:T(8,128)S(1)}) fusion(f32[256,4,1536]{2,1,0:T(4,128)} %reshape.440, f32[256,1536]{1,0:T(8,128)S(1)} %copy-done.16, f32[256,4]{1,0:T(8,128)S(1)} %copy.147), kind=kLoop, calls=%fused_computation.12 | loop fusion | flops 5897216 | bytes 9445376 | tf_op jit(solution)/shard_map/reduce_sum | solution.py:222
  441.2 4.8 convolution_convert_fusion.8
  458.2 3.5 convolution_convert_fusion
  464.9 3.7 convolution_convert_fusion.1
  471.0 7.4 fusion.12
  478.4 7.4 fusion.11
  486.1 7.5 fusion.10
  496.3 54.4 %reduce-scatter.23.cloned.1.call-done = bf16[384,1536]{1,0:T(8,128)(2,1)} async-done(((bf16[1536,1536]{1,0:T(8,128)(2,1)}), bf16[384,1536]{1,0:T(8,128)(2,1)}) %reduce-scatter.23.cloned.1.call-update) | async-done | bytes 1179664 | tf_op jit(solution)/shard_map/reduce_scatter | solution.py:382
  550.7 53.3 %reduce-scatter.17.cloned.1.call-done = bf16[384,1536]{1,0:T(8,128)(2,1)} async-done(((bf16[1536,1536]{1,0:T(8,128)(2,1)}), bf16[384,1536]{1,0:T(8,128)(2,1)}) %reduce-scatter.17.cloned.1.call-update) | async-done | bytes 1179664 | tf_op jit(solution)/shard_map/reduce_scatter | solution.py:373
  604.0 3.8 fusion.78
  610.8 6.6 all-reduce.8
  620.8 4.4 reduce-scatter.25.cloned.1.call-done
  626.2 123.4 %all-reduce.6 = (bf16[384]{0:T(512)(128)(2,1)S(1)}, bf16[384]{0:T(512)(128)(2,1)S(1)}, bf16[384,32]{0,1:T(8,128)(2,1)S(1)}) all-reduce(bf16[384]{0:T(512)(128)(2,1)S(1)} %dynamic-slice.2, bf16[384]{0:T(512)(128)(2,1)S(1)} %dynamic-slice.4, bf16[384,32]{0,1:T(8,128)(2,1)S(1)} %copy.187), channel_id=1, replica_groups=mesh['dp'=4,'expert'=32] {'expert'}, use_global_device_ids=true, to_apply=%region_29.30 | all-reduce | flops 13056 | bytes 52224 | tf_op jit(solution)/shard_map/psum | solution.py:368
  757.9 85.3 %all-reduce.11.cloned.1.call-done = (bf16[384,1536]{1,0:T(8,128)(2,1)}, bf16[384,256]{1,0:T(8,128)(2,1)}, bf16[384,256]{1,0:T(8,128)(2,1)}, bf16[384,1536]{1,0:T(8,128)(2,1)}) async-done(((bf16[384,1536]{1,0:T(8,128)(2,1)}, bf16[384,256]{1,0:T(8,128)(2,1)}, bf16[384,256]{1,0:T(8,128)(2,1)}, bf16[384,1536]{1,0:T(8,128)(2,1)}), (bf16[384,1536]{1,0:T(8,128)(2,1)}, bf16[384,256]{1,0:T(8,128)(2,1)}, ...) | async-done | bytes 2752528 | tf_op jit(solution)/shard_map/psum | solution.py:364
  (283 shorter events, 81.5 us)
Async XLA Ops:
  7.2 3.0 copy-start.48
  7.2 3.3 copy-start.2
  7.2 3.6 copy-start.66
  7.2 3.6 copy-start.67
  7.2 21.4 %copy-start.55 = (bf16[384,32]{0,1:T(8,128)(2,1)S(1)}, bf16[384,32]{0,1:T(8,128)(2,1)}, u32[]{:S(2)}) copy-start(bf16[384,32]{0,1:T(8,128)(2,1)} %param.21) | copy-start | bytes 73732
  7.2 107.1 %all-gather.8.cloned.1.call-start = ((), (), s32[]{:S(2)}) async-start(), calls=%async_computation.12 | async-start | bytes 5898240 | tf_op jit(solution)/shard_map/all_gather | solution.py:118
  8.0 118.4 %all-gather.10.cloned.1.call-start = ((), (), s32[]{:S(2)}) async-start(), calls=%async_computation.13 | async-start | bytes 5898240 | tf_op jit(solution)/shard_map/all_gather | solution.py:121
  8.7 209.4 %all-gather.14.cloned.1.call-start = ((), (), s32[]{:S(2)}) async-start(), calls=%async_computation.15 | async-start | bytes 2949120 | tf_op jit(solution)/shard_map/all_gather | solution.py:128
  10.1 51.9 %copy-start.39 = (bf16[384,256]{1,0:T(8,128)(2,1)S(1)}, bf16[384,256]{1,0:T(8,128)(2,1)}, u32[]{:S(2)}) copy-start(bf16[384,256]{1,0:T(8,128)(2,1)} %param.16) | copy-start | bytes 589828
  10.8 29.7 %copy-start.62 = (f32[256]{0:T(256)}, f32[256]{0:T(256)S(1)}, u32[]{:S(2)}) copy-start(f32[256]{0:T(256)S(1)} %fusion.34) | copy-start | bytes 3076
  10.8 79.5 %copy-start.51 = (f32[256]{0:T(256)}, f32[256]{0:T(256)S(1)}, u32[]{:S(2)}) copy-start(f32[256]{0:T(256)S(1)} %fusion.63) | copy-start | bytes 3076
  52.5 23.3 %copy-start.40 = (bf16[384,256]{1,0:T(8,128)(2,1)S(1)}, bf16[384,256]{1,0:T(8,128)(2,1)}, u32[]{:S(2)}) copy-start(bf16[384,256]{1,0:T(8,128)(2,1)} %param.17) | copy-start | bytes 589828
  52.6 8.7 %copy-start.58 = (s32[1024,1]{0,1:T(1,128)}, s32[1024,1]{0,1:T(1,128)S(1)}, u32[]{:S(2)}) copy-start(s32[1024,1]{0,1:T(1,128)S(1)} %compare_select_fusion) | copy-start | bytes 12292
  74.1 18.2 %copy-start.12 = (bf16[256,1536]{1,0:T(8,128)(2,1)S(1)}, bf16[256,1536]{1,0:T(8,128)(2,1)}, u32[]{:S(2)}) copy-start(bf16[256,1536]{1,0:T(8,128)(2,1)} %param.25) | copy-start | bytes 2359300
  114.3 5.2 copy-start.22
  114.3 5.2 copy-start.24
  114.3 4.8 copy-start.27
  114.3 4.8 copy-start.30
  122.7 3.6 copy-start.3
  123.5 6.6 copy-start.10
  130.9 5.5 copy-start.57
  142.3 67.4 %all-to-all-start = ((bf16[32,40,1536]{2,1,0:T(8,128)(2,1)}), bf16[32,40,1536]{2,1,0:T(8,128)(2,1)}, u32[]{:S(2)}, u32[]{:S(2)}) async-start(bf16[32,40,1536]{2,1,0:T(8,128)(2,1)} %get-tuple-element.90), calls=%async_computation | async-start | bytes 7864320 | tf_op jit(solution)/shard_map/all_to_all | solution.py:198
  162.2 63.9 %all-gather.12.cloned.1.call-start = ((), (), s32[]{:S(2)}) async-start(), calls=%async_computation.14 | async-start | bytes 2949120 | tf_op jit(solution)/shard_map/all_gather | solution.py:127
  209.7 55.5 %all-to-all-start.2 = ((bf16[32,40,1536]{2,1,0:T(8,128)(2,1)}), bf16[32,40,1536]{2,1,0:T(8,128)(2,1)}, u32[]{:S(2)}, u32[]{:S(2)}) async-start(bf16[32,40,1536]{2,1,0:T(8,128)(2,1)} %get-tuple-element.89), calls=%async_computation.2 | async-start | bytes 7864320 | tf_op jit(solution)/shard_map/all_to_all | solution.py:235
  217.5 34.8 %all-gather.16.cloned.1.call-start = ((), (), s32[]{:S(2)}) async-start(), calls=%async_computation.16 | async-start | bytes 2949120 | tf_op jit(solution)/shard_map/all_gather | solution.py:129
  265.2 12.0 %copy-start.69 = (bf16[1,1536,768]{2,1,0:T(8,128)(2,1)S(1)}, bf16[1,1536,768]{2,1,0:T(8,128)(2,1)}, u32[]{:S(2)}) copy-start(bf16[1,1536,768]{2,1,0:T(8,128)(2,1)} %all-gather.16.cloned.1.call-done) | copy-start | bytes 7077892
  277.1 4.9 copy-start.72
  282.0 55.5 %all-to-all-start.1 = ((bf16[32,40,1536]{2,1,0:T(8,128)(2,1)}), bf16[32,40,1536]{2,1,0:T(8,128)(2,1)}, u32[]{:S(2)}, u32[]{:S(2)}) async-start(bf16[32,40,1536]{2,1,0:T(8,128)(2,1)} %bitcast.169), calls=%async_computation.1 | async-start | bytes 7864320 | tf_op jit(solution)/shard_map/all_to_all | solution.py:207
  290.1 5.7 copy-start.68
  290.1 5.7 copy-start.71
  337.6 8.0 copy-start.13
  337.6 55.6 %all-to-all-start.3 = ((bf16[32,40,1536]{2,1,0:T(8,128)(2,1)}), bf16[32,40,1536]{2,1,0:T(8,128)(2,1)}, u32[]{:S(2)}, u32[]{:S(2)}) async-start(bf16[32,40,1536]{2,1,0:T(8,128)(2,1)} %bitcast.168), calls=%async_computation.3 | async-start | bytes 7864320 | tf_op jit(solution)/shard_map/all_to_all | solution.py:264
  345.5 150.0 %reduce-scatter.21.cloned.1.call-start = ((), (), s32[]{:S(2)}) async-start(), calls=%async_computation.22 | async-start | bytes 983040 | tf_op jit(solution)/shard_map/reduce_scatter | solution.py:379
  419.9 18.8 %copy-start.8 = (f32[256,1536]{1,0:T(8,128)S(1)}, f32[256,1536]{1,0:T(8,128)}, u32[]{:S(2)}) copy-start(f32[256,1536]{1,0:T(8,128)} %reduce_sum.175) | copy-start | bytes 4718596
  441.2 7.1 copy-start.1
  450.2 3.4 copy-start.35
  451.7 44.6 %reduce-scatter.19.cloned.1.call-start = ((), (), s32[]{:S(2)}) async-start(), calls=%async_computation.21 | async-start | bytes 983040 | tf_op jit(solution)/shard_map/reduce_scatter | solution.py:376
  458.1 92.6 %reduce-scatter.23.cloned.1.call-start = ((), (), s32[]{:S(2)}) async-start(), calls=%async_computation.23 | async-start | bytes 5898240 | tf_op jit(solution)/shard_map/reduce_scatter | solution.py:382
  461.7 142.2 %reduce-scatter.17.cloned.1.call-start = ((), (), s32[]{:S(2)}) async-start(), calls=%async_computation.20 | async-start | bytes 5898240 | tf_op jit(solution)/shard_map/reduce_scatter | solution.py:373
  468.7 156.5 %reduce-scatter.25.cloned.1.call-start = ((), (), s32[]{:S(2)}) async-start(), calls=%async_computation.24 | async-start | bytes 491520
  470.9 280.5 %reduce-scatter.15.cloned.1.call-start = ((), (), s32[]{:S(2)}) async-start(), calls=%async_computation.19 | async-start | bytes 2949120 | tf_op jit(solution)/shard_map/reduce_scatter | solution.py:284
  478.4 275.2 %reduce-scatter.13.cloned.1.call-start = ((), (), s32[]{:S(2)}) async-start(), calls=%async_computation.18 | async-start | bytes 2949120 | tf_op jit(solution)/shard_map/reduce_scatter | solution.py:281
  485.9 269.8 %reduce-scatter.11.cloned.1.call-start = ((), (), s32[]{:S(2)}) async-start(), calls=%async_computation.17 | async-start | bytes 2949120 | tf_op jit(solution)/shard_map/reduce_scatter | solution.py:278
  493.6 349.6 %all-reduce.11.cloned.1.call-start = ((), (), s32[]{:S(2)}) async-start(), calls=%async_computation.25 | async-start | bytes 5505024 | tf_op jit(solution)/shard_map/psum | solution.py:364
  604.0 3.9 copy-start.20
  609.0 8.7 %copy-start.63 = (f32[256]{0:T(256)S(1)}, f32[256]{0:T(256)}, u32[]{:S(2)}) copy-start(f32[256]{0:T(256)} %copy-done.62) | copy-start | bytes 3076
  609.0 8.7 %copy-start.33 = (bf16[1536,32]{0,1:T(8,128)(2,1)S(1)}, bf16[1536,32]{0,1:T(8,128)(2,1)}, u32[]{:S(2)}) copy-start(bf16[1536,32]{0,1:T(8,128)(2,1)} %copy-done.32) | copy-start | bytes 294916
  843.2 6.5 copy-start.21
  (43 other events, 58.6 us)
Sparse Core Ops, SparseCore 0:
  9.7 56.9 all-gather.7
  68.3 57.9 all-gather.9
  128.0 33.6 all-gather.13
  164.3 32.4 all-gather.11
  219.7 32.5 all-gather.15
  451.8 19.2 reduce-scatter.20
  474.1 22.1 reduce-scatter.18
  498.7 51.9 reduce-scatter.22
  553.1 50.7 reduce-scatter.16
  606.7 18.4 reduce-scatter.24
  627.8 33.6 reduce-scatter.14
  664.4 31.5 reduce-scatter.12
  699.1 31.5 reduce-scatter.10
  734.7 108.4 all-reduce.10
where the time goes:
time: 864 us; the launch traced here: 858 us
  waiting for transfers between devices  348 us (40%)
  blocking collectives  184 us (21%)
  matrix products  108 us (12%)
  local copies, waits for them, and re-layouts  84.7 us (10%)
  other arithmetic  72.6 us (8%)
  starting transfers between devices  45.3 us (5%)
  between operations  15.9 us (2%)
    psum x1, blocking collectives, shards(): lax.psum(layer_grads[4].astype(jnp.bfloat16), 'expert').astype(jnp.float32)  123 us
    psum x1, waiting for transfers between devices, shards(): lax.psum(layer_grads[0].astype(jnp.bfloat16), 'expert').astype(jnp.float32)  85.3 us
    reduce_scatter x1, waiting for transfers between devices, shards(): lax.psum_scatter(summed[3].astype(jnp.bfloat16), 'dp', scatter_dimension=...  54.4 us
    reduce_scatter x1, waiting for transfers between devices, shards(): lax.psum_scatter(summed[0].astype(jnp.bfloat16), 'dp', scatter_dimension=...  53.3 us
    all_to_all x1, waiting for transfers between devices, shards(): lax.all_to_all(send_rows, 'expert', split_axis=0, concat_axis=0, tiled=True)  47 us
    all_to_all x1, waiting for transfers between devices, shards(): lax.all_to_all(by_source(produced, local_experts, item_count), 'expert',...  36.8 us
    all_to_all x1, waiting for transfers between devices, shards(): lax.all_to_all(by_source(row_back, local_experts, capacity), 'expert', sp...  29 us
    dot_general x10, matrix products, contract(): lax.dot_general(left_side, right_side, (((left_dim,), (right_dim,)), ((),...  24.3 us
  transfers between devices with their start and end apart: 18, of which 11 were waited for; matrix products, arithmetic and copies ran while one was open for 20% of the time, Pallas kernels for 0%

commit v1 on v0

v1 whole, which is shorter than its diff:
```python
import functools
import itertools

import jax
import jax.numpy as jnp
import numpy as np
from jax import lax
from jax.experimental import pallas as pl
from jax.experimental.pallas import tpu as pltpu
from jax.sharding import PartitionSpec as P

MODEL_WIDTH = 1536
QUERY_HEADS = 12
KEY_VALUE_HEADS = 2
HEAD_SIZE = 128
TOPK = 4
SEQ = 256
EXPERTS = 32
CAP = 40
FF = 768
KV = KEY_VALUE_HEADS * HEAD_SIZE
SHARD = MODEL_WIDTH // 4
HALF = SHARD // 2
QUARTER = HALF // 2
EPSILON = 1e-06
ROPE_BASE = 10000.0
SCALE = HEAD_SIZE ** (-0.5)
MESH = pl.DeviceIdType.MESH
F32 = jnp.float32
BF16 = jnp.bfloat16
VMEM = pltpu.VMEM
ANY = pl.ANY
LIMIT = 60 * 1024 * 1024


def _offsets():
    def far(a):
        return min(a, 4 - a)

    every = [o for o in itertools.product(range(4), range(4), range(2)) if o != (0, 0, 0)]
    return sorted(every, key=lambda o: (far(o[0]) + far(o[1]), o))[::-1]


OFFSETS = _offsets()


def rope_tables():
    position = np.arange(SEQ, dtype=np.float32)
    frequency = (
        np.float32(ROPE_BASE) ** (-np.arange(64, dtype=np.float32) * np.float32(2.0 / HEAD_SIZE))
    ).astype(np.float32)
    angles = (position[:, None] * frequency[None, :]).astype(np.float32)
    cosine = np.cos(angles.astype(np.float64)).astype(np.float32)
    sine = np.sin(angles.astype(np.float64)).astype(np.float32)
    return (
        np.concatenate([cosine, cosine], axis=1),
        np.concatenate([-sine, sine], axis=1),
    )


def mm(left, right, left_dim=1, right_dim=0):
    return lax.dot_general(
        left, right, (((left_dim,), (right_dim,)), ((), ())), preferred_element_type=F32
    )


class Place:
    def __init__(self):
        self.x = lax.axis_index("dp")
        self.e = lax.axis_index("expert")
        self.core = lax.rem(self.e, 2)
        self.y = lax.rem(self.e // 2, 4)
        self.z = self.e // 8
        self.xl = lax.rem(self.x + 3, 4)
        self.xr = lax.rem(self.x + 1, 4)
        self.x2 = lax.rem(self.x + 2, 4)
        self.left = (self.xl, self.e)
        self.right = (self.xr, self.e)
        self.across = (self.x2, self.e)
        self.sibling = (self.x, self.e + 1 - 2 * self.core)

    def peer(self, offset):
        dz, dy, dc = offset
        return (
            lax.rem(self.z + dz, 4) * 8 + lax.rem(self.y + dy, 4) * 2 + lax.rem(self.core + dc, 2)
        )

    def peers(self):
        return [self.peer(o) for o in OFFSETS]


def greet(devices):
    barrier = pltpu.get_barrier_semaphore()
    for d in devices:
        pl.semaphore_signal(barrier, inc=1, device_id=d, device_id_type=MESH)
    return barrier


def remote(src, dst, send, recv, device):
    return pltpu.make_async_remote_copy(
        src_ref=src, dst_ref=dst, send_sem=send, recv_sem=recv, device_id=device, device_id_type=MESH
    )


def rows(start, count, align=16):
    return pl.ds(pl.multiple_of(start, align), count)


class Gather:
    def __init__(self, place, shard, full, send, recv):
        p = place
        half = p.core * HALF
        other = HALF - half

        def region(x, first, count):
            return full.at[rows(x * SHARD + first, count, 32)]

        def move(k, src, dst, device):
            return remote(src, dst, send.at[k], recv.at[k], device)

        mine = shard.at[rows(half, HALF, 32)]
        self.direct = [
            move(0, mine, region(p.x, half, HALF), p.right),
            move(1, mine, region(p.x, half, HALF), p.left),
        ]
        from_left = region(p.xl, half, QUARTER)
        from_right = region(p.xr, half + QUARTER, QUARTER)
        self.forward = [
            move(2, from_left, from_left, p.right),
            move(3, from_right, from_right, p.left),
        ]
        whole_left = region(p.xl, half, HALF)
        whole_right = region(p.xr, half, HALF)
        far_one = region(p.x2, half, QUARTER)
        far_two = region(p.x2, half + QUARTER, QUARTER)
        self.near = [
            move(4, whole_left, whole_left, p.sibling),
            move(5, whole_right, whole_right, p.sibling),
        ]
        self.far = [
            move(6, far_one, far_one, p.sibling),
            move(7, far_two, far_two, p.sibling),
        ]

    def start(self):
        for c in self.direct:
            c.start()

    def relay(self):
        for k in range(2):
            self.direct[k].wait_recv()
            self.forward[k].start()
            self.near[k].start()

    def relay_far(self):
        for k in range(2):
            self.forward[k].wait_recv()
            self.far[k].start()

    def arrived_near(self):
        for c in self.near:
            c.wait_recv()

    def arrived_far(self):
        for c in self.far:
            c.wait_recv()

    def finish(self):
        for c in self.direct + self.forward + self.near + self.far:
            c.wait_send()


def slot_rows(posm_ref, first, count):
    slot = lax.broadcasted_iota(jnp.int32, (CAP, SEQ), 0).astype(F32)
    return [
        jnp.where(posm_ref[pl.ds(first + j, 1), :] == slot, 1.0, 0.0) for j in range(count)
    ]


def turn(values, cosine, sine):
    return values * cosine + pltpu.roll(values, 64, 1) * sine


def turn_back(values, cosine, sine):
    return values * cosine - pltpu.roll(values, 64, 1) * sine


def softmax_parts(q_head, k_head, causal):
    scores = mm(q_head, k_head, 1, 1) * SCALE
    scores = jnp.where(causal, scores, -jnp.inf)
    largest = jnp.max(scores, axis=-1, keepdims=True)
    exponent = jnp.exp(scores - largest)
    return exponent / jnp.sum(exponent, axis=-1, keepdims=True)


def causal_mask():
    row = lax.broadcasted_iota(jnp.int32, (SEQ, SEQ), 0)
    column = lax.broadcasted_iota(jnp.int32, (SEQ, SEQ), 1)
    return column <= row


def front_kernel(
    tokens, cotangent, routes, small, wq, wkv, wo, cosine, sine,
    dy_in, wq_full, wkv_full, wo_full, small_all, posm, share, n1, q, kv, o, r, n2,
    dy_out, wqf, wkvf, wof, qacc, kvacc, racc,
    gs, gr, ss, sr, as_, ar, ls,
):
    p = Place()
    peers = p.peers()
    barrier = greet([p.left, p.right, p.across] + [(p.x, t) for t in peers])

    lane = lax.broadcasted_iota(jnp.int32, (EXPERTS, SEQ), 0)
    named = routes[0:1, :] == lane
    for j in range(1, TOPK):
        named = jnp.logical_or(named, routes[j : j + 1, :] == lane)
    earlier = (
        lax.broadcasted_iota(jnp.int32, (SEQ, SEQ), 0)
        < lax.broadcasted_iota(jnp.int32, (SEQ, SEQ), 1)
    ).astype(F32).astype(BF16)
    place_of = mm(named.astype(F32).astype(BF16), earlier)
    posm[...] = jnp.where(named, place_of, -1.0)

    small_all[p.x] = small[...]
    pl.semaphore_wait(barrier, len(peers) + 3)

    small_moves = [
        remote(small, small_all.at[p.x], ss.at[k], sr.at[k], d)
        for k, d in enumerate([p.right, p.left, p.across])
    ]
    for c in small_moves:
        c.start()
    gq = Gather(p, wq, wqf, gs.at[0], gr.at[0])
    gkv = Gather(p, wkv, wkvf, gs.at[1], gr.at[1])
    go = Gather(p, wo, wof, gs.at[2], gr.at[2])
    gq.start()
    gkv.start()

    mine = [
        pltpu.make_async_copy(w, f.at[rows(p.x * SHARD, SHARD, 128)], ls.at[k])
        for k, (w, f) in enumerate([(wq, wqf), (wkv, wkvf), (wo, wof)])
    ]
    for c in mine:
        c.start()

    x = tokens[...].astype(F32)
    unit = x * lax.rsqrt(jnp.mean(x * x, axis=-1, keepdims=True) + EPSILON)
    for c in small_moves:
        c.wait_recv()
    for s in range(4):
        cut = slice(s * SHARD, (s + 1) * SHARD)
        n1[:, cut] = (unit[:, cut] * small_all[s, 32:33, :].astype(F32)).astype(BF16)
    logits = mm(small_all[0, 0:32, :], tokens[:, 0:SHARD], 1, 1)
    for s in range(1, 4):
        logits += mm(small_all[s, 0:32, :], tokens[:, s * SHARD : (s + 1) * SHARD], 1, 1)
    top = jnp.max(jnp.where(named, logits, -jnp.inf), axis=0, keepdims=True)
    weight = jnp.where(named, jnp.exp(jnp.minimum(logits - top, 0.0)), 0.0)
    share[...] = weight / jnp.sum(weight, axis=0, keepdims=True)

    @pl.loop(0, EXPERTS // 4)
    def _(i):
        blocks = slot_rows(posm, i * 4, 4)
        gain = jnp.concatenate(
            [
                jnp.sum(b * share[pl.ds(i * 4 + j, 1), :], axis=-1, keepdims=True)
                for j, b in enumerate(blocks)
            ],
            axis=0,
        )
        picked = mm(jnp.concatenate(blocks, axis=0).astype(BF16), cotangent[...])
        dy_out[pl.ds(i * 4, 4)] = (picked * gain).reshape(4, CAP, MODEL_WIDTH).astype(BF16)

    sends = [
        remote(dy_out.at[t], dy_in.at[p.e], as_.at[k], ar.at[k], (p.x, t))
        for k, t in enumerate(peers)
    ]
    for c in sends:
        c.start()
    own_dy = pltpu.make_async_copy(dy_out.at[p.e], dy_in.at[p.e], ls.at[3])
    own_dy.start()

    def part(x_index):
        return n1[:, rows(x_index * SHARD, SHARD, 128)]

    def block(full, x_index):
        return full[rows(x_index * SHARD, SHARD, 128), :]

    own = part(p.x)
    qacc[...] = mm(own, wq[...])
    kvacc[...] = mm(own, wkv[...])
    gq.relay()
    gkv.relay()
    go.start()
    gq.arrived_near()
    gkv.arrived_near()
    for s in (p.xl, p.xr):
        qacc[...] += mm(part(s), block(wqf, s))
        kvacc[...] += mm(part(s), block(wkvf, s))
    gq.relay_far()
    gkv.relay_far()
    gq.arrived_far()
    gkv.arrived_far()
    qacc[...] += mm(part(p.x2), block(wqf, p.x2))
    kvacc[...] += mm(part(p.x2), block(wkvf, p.x2))
    for c in mine:
        c.wait()
    keep = [
        pltpu.make_async_copy(f, out, ls.at[4 + k])
        for k, (f, out) in enumerate([(wqf, wq_full), (wkvf, wkv_full), (wof, wo_full)])
    ]
    keep[0].start()
    keep[1].start()

    cos = cosine[...]
    sin = sine[...]
    for h in range(KEY_VALUE_HEADS):
        cut = slice(h * HEAD_SIZE, (h + 1) * HEAD_SIZE)
        kv[:, cut] = turn(kvacc[:, cut], cos, sin).astype(BF16)
        cut = slice(KV + h * HEAD_SIZE, KV + (h + 1) * HEAD_SIZE)
        kv[:, cut] = kvacc[:, cut].astype(BF16)
    causal = causal_mask()
    for h in range(QUERY_HEADS):
        cut = slice(h * HEAD_SIZE, (h + 1) * HEAD_SIZE)
        c = h // (QUERY_HEADS // KEY_VALUE_HEADS)
        q_head = turn(qacc[:, cut], cos, sin).astype(BF16)
        q[:, cut] = q_head
        weights = softmax_parts(q_head, kv[:, c * HEAD_SIZE : (c + 1) * HEAD_SIZE], causal)
        o[:, cut] = mm(
            weights.astype(BF16), kv[:, KV + c * HEAD_SIZE : KV + (c + 1) * HEAD_SIZE]
        ).astype(BF16)

    def opart(x_index):
        return o[:, rows(x_index * SHARD, SHARD, 128)]

    racc[...] = tokens[...].astype(F32) + mm(opart(p.x), wo[...])
    go.relay()
    go.arrived_near()
    for s in (p.xl, p.xr):
        racc[...] += mm(opart(s), block(wof, s))
    go.relay_far()
    go.arrived_far()
    keep[2].start()
    residual = racc[...] + mm(opart(p.x2), block(wof, p.x2))
    r[...] = residual
    unit = residual * lax.rsqrt(jnp.mean(residual * residual, axis=-1, keepdims=True) + EPSILON)
    for s in range(4):
        cut = slice(s * SHARD, (s + 1) * SHARD)
        n2[:, cut] = (unit[:, cut] * small_all[s, 33:34, :].astype(F32)).astype(BF16)

    for c in sends:
        c.wait()
    own_dy.wait()
    for c in small_moves:
        c.wait_send()
    for g in (gq, gkv, go):
        g.finish()
    for c in keep:
        c.wait()


def front(tokens, cotangent, routes, small, wq, wkv, wo):
    cosine, sine = rope_tables()
    D = MODEL_WIDTH

    def arr(shape, dtype=BF16):
        return jax.ShapeDtypeStruct(shape, dtype)

    outs = [
        arr((EXPERTS, CAP, D)), arr((D, D)), arr((D, 2 * KV)), arr((D, D)), arr((4, 48, SHARD)),
        arr((EXPERTS, SEQ), F32), arr((EXPERTS, SEQ), F32), arr((SEQ, D)), arr((SEQ, D)),
        arr((SEQ, 2 * KV)), arr((SEQ, D)), arr((SEQ, D), F32), arr((SEQ, D)),
    ]
    vm = pl.BlockSpec(memory_space=VMEM)
    hb = pl.BlockSpec(memory_space=ANY)
    sem = pltpu.SemaphoreType.DMA
    return pl.pallas_call(
        front_kernel,
        out_shape=outs,
        in_specs=[vm] * 9,
        out_specs=[hb] * 4 + [vm] * 9,
        scratch_shapes=[
            VMEM((EXPERTS, CAP, D), BF16),
            VMEM((D, D), BF16),
            VMEM((D, 2 * KV), BF16),
            VMEM((D, D), BF16),
            VMEM((SEQ, D), F32),
            VMEM((SEQ, 2 * KV), F32),
            VMEM((SEQ, D), F32),
            sem((3, 8)),
            sem((3, 8)),
            sem((3,)),
            sem((3,)),
            sem((31,)),
            sem((31,)),
            sem((7,)),
        ],
        compiler_params=pltpu.CompilerParams(
            collective_id=0, has_side_effects=True, vmem_limit_bytes=LIMIT
        ),
        name="front",
    )(tokens, cotangent, routes, small, wq, wkv, wo, jnp.asarray(cosine), jnp.asarray(sine))


def norm_back(v, gain, grad):
    scale = lax.rsqrt(jnp.mean(v * v, axis=-1, keepdims=True) + EPSILON)
    unit = v * scale
    w = grad * gain
    return (
        (w - unit * jnp.mean(w * unit, axis=-1, keepdims=True)) * scale,
        jnp.sum(grad * unit, axis=0),
    )


def gelu_parts(a):
    inner = jnp.tanh(0.7978845608028654 * (a + 0.044715 * a * a * a))
    value = 0.5 * a * (1.0 + inner)
    slope = 0.5 * (1.0 + inner) + 0.5 * a * (1.0 - inner * inner) * 0.7978845608028654 * (
        1.0 + 3.0 * 0.044715 * a * a
    )
    return value, slope


def exchange(v):
    return lax.all_to_all(v, "expert", split_axis=0, concat_axis=0, tiled=True)


def pack_small(w_router, norm_one, norm_two):
    return jnp.concatenate(
        [w_router.T, norm_one[None], norm_two[None], jnp.zeros((14, SHARD), BF16)], axis=0
    )


def shards(
    tokens, routes, w_query, key_matrix, value_matrix, w_output, norm_one, norm_two,
    w_router, w_gate, w_up, w_down, cotangent,
):
    small = pack_small(w_router, norm_one, norm_two)
    wkv = jnp.concatenate([key_matrix, value_matrix], axis=1)
    (dy, fq, fkv, fo, small_all, posm, share, n1, q, kv, o, r, n2) = front(
        tokens, cotangent, routes.T, small, w_query, wkv, w_output
    )
    gate = lax.all_gather(w_gate[0], "dp", axis=0, tiled=True)
    up = lax.all_gather(w_up[0], "dp", axis=0, tiled=True)
    down = lax.all_gather(w_down[0], "dp", axis=0, tiled=True)
    D = (posm[:, None, :] == jnp.arange(CAP, dtype=F32)[None, :, None]).astype(BF16)
    D = D.reshape(EXPERTS * CAP, SEQ)
    N = EXPERTS * CAP
    R = exchange(mm(D, n2).astype(BF16).reshape(EXPERTS, CAP, MODEL_WIDTH)).reshape(N, MODEL_WIDTH)
    dy = dy.reshape(N, MODEL_WIDTH)
    a = mm(R, gate)
    b = mm(R, up)
    value, slope = gelu_parts(a)
    hid = (value * b).astype(BF16)
    y = mm(hid, down, 1, 1).astype(BF16)
    y = exchange(y.reshape(EXPERTS, CAP, MODEL_WIDTH)).reshape(N, MODEL_WIDTH)
    dh = mm(dy, down)
    da = (dh * b * slope).astype(BF16)
    db = (dh * value).astype(BF16)
    dR = (mm(da, gate, 1, 1) + mm(db, up, 1, 1)).astype(BF16)
    dR = exchange(dR.reshape(EXPERTS, CAP, MODEL_WIDTH)).reshape(N, MODEL_WIDTH)

    def scatter(v):
        return lax.psum_scatter(v.astype(BF16), "dp", scatter_dimension=0, tiled=True).astype(F32)

    g_gate = scatter(mm(R, da, 0, 0))[None]
    g_up = scatter(mm(R, db, 0, 0))[None]
    g_down = scatter(mm(dy, hid, 0, 0))[None]

    dz = cotangent.astype(F32)
    gain_one = small_all[:, 32].reshape(-1).astype(F32)
    gain_two = small_all[:, 33].reshape(-1).astype(F32)
    router = jnp.transpose(small_all[:, :32], (0, 2, 1)).reshape(MODEL_WIDTH, EXPERTS)
    gslot = jnp.sum(D.reshape(EXPERTS, CAP, SEQ).astype(F32) * share[:, None, :], axis=-1)
    weighted = (D.reshape(EXPERTS, CAP, SEQ).astype(F32) * share[:, None, :]).reshape(N, SEQ)
    hi = weighted.astype(BF16)
    lo = (weighted - hi.astype(F32)).astype(BF16)
    mixed = (r + (mm(hi, y, 0, 0) + mm(lo, y, 0, 0))).astype(BF16)
    dslot = jnp.sum(mm(D, cotangent) * y.astype(F32), axis=-1).reshape(EXPERTS, CAP)
    dg = jnp.sum(D.reshape(EXPERTS, CAP, SEQ).astype(F32) * dslot[:, :, None], axis=1)
    dl = share * (dg - jnp.sum(share * dg, axis=0, keepdims=True))
    dlogits = jnp.where(posm >= 0, dl, 0.0).astype(BF16)
    g_router = mm(tokens, dlogits, 0, 1)
    dn2 = mm(D, dR, 0, 0)
    back, g_two = norm_back(r, gain_two, dn2)
    dr = dz + back
    dA = dr.astype(BF16)
    g_out = mm(o, dA, 0, 0)
    do = mm(dA, fo, 1, 1).astype(BF16)
    cosine, sine = rope_tables()
    causal = causal_mask()
    dqs, dks, dvs = [], [], []
    for c in range(KEY_VALUE_HEADS):
        dk = 0.0
        dv = 0.0
        k_head = kv[:, c * 128 : (c + 1) * 128]
        v_head = kv[:, KV + c * 128 : KV + (c + 1) * 128]
        for h in range(c * 6, c * 6 + 6):
            cut = slice(h * 128, (h + 1) * 128)
            pf = softmax_parts(q[:, cut], k_head, causal)
            dp = mm(do[:, cut], v_head, 1, 1)
            ds = (pf * (dp - jnp.sum(pf * dp, axis=-1, keepdims=True))).astype(BF16)
            dq = mm(ds, k_head) * SCALE
            dqs.append((dq * cosine - jnp.roll(dq, 64, 1) * sine).astype(BF16))
            dk += mm(ds, q[:, cut], 0, 0)
            dv += mm(pf.astype(BF16), do[:, cut], 0, 0)
        dk = dk * SCALE
        dks.append((dk * cosine - jnp.roll(dk, 64, 1) * sine).astype(BF16))
        dvs.append(dv.astype(BF16))
    dqp = jnp.concatenate(dqs, axis=1)
    dkvp = jnp.concatenate(dks + dvs, axis=1)
    dn1 = mm(dqp, fq, 1, 1) + mm(dkvp, fkv, 1, 1)
    g_q = mm(n1, dqp, 0, 0)
    g_kv = mm(n1, dkvp, 0, 0)
    back, g_one = norm_back(tokens.astype(F32), gain_one, dn1)
    g_tok = dr + back + mm(dlogits, router, 0, 1)
    g_small = jnp.concatenate([g_router.T, g_one[None], g_two[None]], axis=0)
    whole = jnp.concatenate([g_q, g_kv, g_out, g_small.T], axis=1).astype(BF16)
    part = lax.psum_scatter(whole, "dp", scatter_dimension=0, tiled=True)
    part = lax.psum(part, "expert").astype(F32)
    D_ = MODEL_WIDTH
    return (
        mixed,
        g_tok,
        part[:, :D_],
        part[:, D_ : D_ + KV],
        part[:, D_ + KV : D_ + 2 * KV],
        part[:, D_ + 2 * KV : 2 * D_ + 2 * KV],
        part[:, 2 * D_ + 2 * KV + 32],
        part[:, 2 * D_ + 2 * KV + 33],
        part[:, 2 * D_ + 2 * KV : 2 * D_ + 2 * KV + 32],
        g_gate,
        g_up,
        g_down,
    )


def solution(mesh):
    rows_split = P(("dp", "expert"), None)
    flat = P("dp", None)
    vector = P("dp")
    owned = P("expert", "dp", None)
    return jax.shard_map(
        shards,
        mesh=mesh,
        in_specs=(
            rows_split, rows_split, flat, flat, flat, flat, vector, vector, flat, owned, owned, owned,
            rows_split,
        ),
        out_specs=(
            rows_split, rows_split, flat, flat, flat, flat, vector, vector, flat, owned, owned, owned,
        ),
        check_vma=False,
    )
```

time: 864 us -> 719 us (0.83)
  blocking collectives: 184 us -> 0 us
  Pallas kernels: 0 us -> 98.7 us
  other arithmetic: 72.6 us -> 31.3 us
  local copies, waits for them, and re-layouts: 84.7 us -> 45.3 us
  waiting for transfers between devices: 348 us -> 376 us
  starting transfers between devices: 45.3 us -> 20.8 us
  matrix products: 108 us -> 121 us
    psum x1 -> x0, blocking collectives: 123 us -> none  [shards(): lax.psum(layer_grads[4].astype(jnp.bfloat16), 'expert').astype(jnp.float32)]
    pallas_call x0 -> x1, Pallas kernels: none -> 98.7 us  [front(): pl.pallas_call(front_kernel, out_shape=outs, in_specs=[vm] * 9, out_specs...]
    unnamed x15 -> x9, waiting for transfers between devices: 7.19 us -> 73.6 us
    all_gather x5 -> x0, blocking collectives: 53.5 us -> none  [the longest x1 14.4 us: shards(): lax.all_gather(value_matrix, 'dp', axis=0, tiled=True)]
    gather x4 -> x0, local copies, waits for them, and re-layouts: 30.9 us -> none  [the longest x1 9.9 us: shards(): returned_grads.reshape(experts * capacity, MODEL_WIDTH)[target]]
    psum x1, waiting for transfers between devices: 85.3 us -> 110 us  [shards(): part = lax.psum(part, 'expert').astype(F32)]
    all_to_all x4 -> x3, waiting for transfers between devices: 126 us -> 101 us  [exchange(): return lax.all_to_all(v, 'expert', split_axis=0, concat_axis=0, tiled=True)]
    all_to_all x4 -> x3, starting transfers between devices: 43.6 us -> 19.8 us  [exchange(): return lax.all_to_all(v, 'expert', split_axis=0, concat_axis=0, tiled=True)]
  transfers between devices with their start and end apart: 18 -> 11, of which waited for: 11 -> 8; matrix products, arithmetic and copies ran while one was open for 20% -> 15% of each run, Pallas kernels for 0% -> 14%
where the time goes in v1:
time: 719 us; the launch traced here: 709 us
  waiting for transfers between devices  376 us (52%)
  matrix products  121 us (17%)
  Pallas kernels  98.7 us (14%)
  local copies, waits for them, and re-layouts  45.3 us (6%)
  other arithmetic  31.3 us (4%)
  starting transfers between devices  20.8 us (3%)
  between operations  16.3 us (2%)
    dot_general x82, matrix products, mm(): lax.dot_general(left, right, (((left_dim,), (right_dim,)), ((), ())), pre...  121 us
    psum x1, waiting for transfers between devices, shards(): part = lax.psum(part, 'expert').astype(F32)  110 us
    all_to_all x3, waiting for transfers between devices, exchange(): return lax.all_to_all(v, 'expert', split_axis=0, concat_axis=0, tiled=True)  101 us
    pallas_call x1, Pallas kernels, front(): pl.pallas_call(front_kernel, out_shape=outs, in_specs=[vm] * 9, out_specs...  98.7 us
    reduce_scatter x3, waiting for transfers between devices, scatter(): lax.psum_scatter(v.astype(BF16), 'dp', scatter_dimension=0, tiled=True)  91.3 us
    unnamed x9, waiting for transfers between devices  73.6 us
    unnamed x189, local copies, waits for them, and re-layouts  34.7 us
    all_to_all x3, starting transfers between devices, exchange(): return lax.all_to_all(v, 'expert', split_axis=0, concat_axis=0, tiled=True)  19.8 us
  transfers between devices with their start and end apart: 11, of which 8 were waited for; matrix products, arithmetic and copies ran while one was open for 15% of the time, Pallas kernels for 14%

profile of v1, /device:TPU:1, one launch (start us, length us, event | category | flops | bytes accessed | tf_op | source)
XLA Modules:
  0.0 709.4 jit_solution(121926985916875772)
XLA Ops:
  10.2 1.8 pad_maximum_fusion.1.wkv
  12.0 1.4 maximum_maximum_fusion.small
  13.4 98.7 %front.1 = (bf16[32,40,1536]{2,1,0:T(8,128)(2,1)}, bf16[1536,1536]{1,0:T(8,128)(2,1)}, bf16[1536,512]{1,0:T(8,128)(2,1)}, bf16[1536,1536]{1,0:T(8,128)(2,1)}, bf...) custom-call(bf16[256,1536]{1,0:T(8,128)(2,1)} %tokens.1, ...), custom_call_target="tpu_custom_call" | custom-call | tf_op jit(solution)/shard_map/front/pallas_call | solution.py:375
  113.2 4.4 convolution_convert_fusion.3
  117.6 4.8 all-to-all-start
  128.7 41.1 %all-to-all-done = bf16[32,40,1536]{2,1,0:T(8,128)(2,1)} async-done(((bf16[32,40,1536]{2,1,0:T(8,128)(2,1)}), bf16[32,40,1536]{2,1,0:T(8,128)(2,1)}, u32[]{:S(2)}, u32[]{:S(2)}) %all-to-all-start) | async-done | bytes 3932192 | tf_op jit(solution)/shard_map/all_to_all | solution.py:423
  169.9 8.1 %fusion.19 = f32[1280,768]{1,0:T(8,128)} fusion(bf16[1280,1536]{1,0:T(8,128)(2,1)} %bitcast.4, bf16[1,1536,768]{2,1,0:T(8,128)(2,1)} %all-gather.7.cloned.1.call-done), kind=kOutput, calls=%fused_computation.41 | convolution fusion | flops 3019898880 | bytes 10223616 | tf_op jit(solution)/shard_map/dot_general | solution.py:62
  178.0 7.9 %fusion.15 = f32[1280,768]{1,0:T(8,128)} fusion(bf16[1280,1536]{1,0:T(8,128)(2,1)} %bitcast.4, bf16[1,1536,768]{2,1,0:T(8,128)(2,1)} %all-gather.9.cloned.1.call-done), kind=kOutput, calls=%fused_computation.37 | convolution fusion | flops 3019898880 | bytes 10223616 | tf_op jit(solution)/shard_map/dot_general | solution.py:62
  185.9 11.0 %multiply_convert_fusion = (bf16[1280,768]{1,0:T(8,128)(2,1)S(1)}, bf16[1280,768]{1,0:T(8,128)(2,1)S(1)}, bf16[1280,768]{1,0:T(8,128)(2,1)}) fusion(f32[1280,768]{1,0:T(8,128)} %fusion.19, f32[1280,768]{1,0:T(8,128)} %fusion.15, bf16[1280,1536]{1,0:T(8,128)(2,1)} %bitcast.117, bf16[1,1536,768]{2,1,0:T(8,128)(2,1)} %all-gather.11.cloned.1.call-done), kind=kOutput, calls=%fused_computation.17 | convolution fusion | flops 3044474880 | bytes 20054016 | tf_op jit(solution)/shard_map/dot_general | solution.py:62
  197.0 3.3 fusion.17
  200.3 5.0 fusion
  205.3 7.2 %all-to-all-start.2 = ((bf16[32,40,1536]{2,1,0:T(8,128)(2,1)}), bf16[32,40,1536]{2,1,0:T(8,128)(2,1)}, u32[]{:S(2)}, u32[]{:S(2)}) async-start(bf16[32,40,1536]{2,1,0:T(8,128)(2,1)} %bitcast.113), calls=%async_computation.2 | async-start | bytes 7864320 | tf_op jit(solution)/shard_map/all_to_all | solution.py:423
  219.2 1.5 fusion.276
  227.2 4.8 convolution_convert_fusion.2
  232.1 28.1 %all-to-all-done.2 = bf16[32,40,1536]{2,1,0:T(8,128)(2,1)} async-done(((bf16[32,40,1536]{2,1,0:T(8,128)(2,1)}), bf16[32,40,1536]{2,1,0:T(8,128)(2,1)}, u32[]{:S(2)}, u32[]{:S(2)}) %all-to-all-start.2) | async-done | bytes 3932192 | tf_op jit(solution)/shard_map/all_to_all | solution.py:423
  260.2 7.9 %all-to-all-start.1 = ((bf16[32,40,1536]{2,1,0:T(8,128)(2,1)}), bf16[32,40,1536]{2,1,0:T(8,128)(2,1)}, u32[]{:S(2)}, u32[]{:S(2)}) async-start(bf16[32,40,1536]{2,1,0:T(8,128)(2,1)} %bitcast.112), calls=%async_computation.1 | async-start | bytes 7864320 | tf_op jit(solution)/shard_map/all_to_all | solution.py:423
  268.3 4.3 multiply_reduce_fusion
  273.1 3.8 convolution_convert_fusion.8
  278.1 1.7 fusion.198
  280.3 1.7 fusion.185
  283.6 32.1 %all-to-all-done.1 = bf16[32,40,1536]{2,1,0:T(8,128)(2,1)} async-done(((bf16[32,40,1536]{2,1,0:T(8,128)(2,1)}), bf16[32,40,1536]{2,1,0:T(8,128)(2,1)}, u32[]{:S(2)}, u32[]{:S(2)}) %all-to-all-start.1) | async-done | bytes 3932192 | tf_op jit(solution)/shard_map/all_to_all | solution.py:423
  315.7 3.5 fusion.21
  338.1 1.4 copy-done.79
  339.6 1.6 fusion.279
  341.2 1.4 convolution_convert_fusion.1
  344.1 1.9 fusion.29
  346.2 1.5 convolution_convert_fusion
  347.7 5.2 pad_maximum_fusion
  352.9 14.7 %copy.187 = bf16[1536,3618]{1,0:T(8,128)(2,1)} copy(bf16[1536,3618]{0,1:T(8,128)(2,1)} %pad_maximum_fusion) | data formatting | bytes 22228992
  367.6 7.4 %convolution_convert_fusion.6 = bf16[1536,768]{1,0:T(8,128)(2,1)} fusion(bf16[1280,1536]{1,0:T(8,128)(2,1)} %bitcast.4, bf16[1280,768]{1,0:T(8,128)(2,1)} %copy-done.88), kind=kOutput, calls=%fused_computation.22 | convolution fusion | flops 3021078528 | bytes 8257536 | tf_op jit(solution)/shard_map/dot_general | solution.py:62
  375.1 7.9 %convolution_convert_fusion.5 = bf16[1536,768]{1,0:T(8,128)(2,1)} fusion(bf16[1280,1536]{1,0:T(8,128)(2,1)} %bitcast.4, bf16[1280,768]{1,0:T(8,128)(2,1)} %copy-done.90), kind=kOutput, calls=%fused_computation.21 | convolution fusion | flops 3021078528 | bytes 8257536 | tf_op jit(solution)/shard_map/dot_general | solution.py:62
  383.4 7.4 %convolution_convert_fusion.4 = bf16[1536,768]{1,0:T(8,128)(2,1)} fusion(bf16[1280,1536]{1,0:T(8,128)(2,1)} %bitcast.118, bf16[1280,768]{1,0:T(8,128)(2,1)} %get-tuple-element.84), kind=kOutput, calls=%fused_computation.20 | convolution fusion | flops 3021078528 | bytes 8257536 | tf_op jit(solution)/shard_map/dot_general | solution.py:62
  391.8 3.4 convolution_bitcast_fusion.1
  395.2 4.2 fusion.10
  399.4 71.6 %reduce-scatter.13.cloned.1.call-done = bf16[384,3618]{1,0:T(8,128)(2,1)} async-done(((bf16[1536,3618]{1,0:T(8,128)(2,1)}), bf16[384,3618]{1,0:T(8,128)(2,1)}) %reduce-scatter.13.cloned.1.call-update) | async-done | bytes 2778640
  471.1 4.5 copy.188
  475.6 3.1 convolution_add_fusion.1
  478.7 26.9 %reduce-scatter.7.cloned.1.call-done = bf16[384,768]{1,0:T(8,128)(2,1)} async-done(((bf16[1536,768]{1,0:T(8,128)(2,1)}), bf16[384,768]{1,0:T(8,128)(2,1)}) %reduce-scatter.7.cloned.1.call-update) | async-done | bytes 589840 | tf_op jit(solution)/shard_map/reduce_scatter | solution.py:462
  505.6 2.2 bitcast_convert_fusion.2
  507.8 32.4 %reduce-scatter.9.cloned.1.call-done = bf16[384,768]{1,0:T(8,128)(2,1)} async-done(((bf16[1536,768]{1,0:T(8,128)(2,1)}), bf16[384,768]{1,0:T(8,128)(2,1)}) %reduce-scatter.9.cloned.1.call-update) | async-done | bytes 589840 | tf_op jit(solution)/shard_map/reduce_scatter | solution.py:462
  540.1 2.2 bitcast_convert_fusion.1
  542.3 32.0 %reduce-scatter.11.cloned.1.call-done = bf16[384,768]{1,0:T(8,128)(2,1)} async-done(((bf16[1536,768]{1,0:T(8,128)(2,1)}), bf16[384,768]{1,0:T(8,128)(2,1)}) %reduce-scatter.11.cloned.1.call-update) | async-done | bytes 589840 | tf_op jit(solution)/shard_map/reduce_scatter | solution.py:462
  574.3 2.2 bitcast_convert_fusion
  576.4 110.2 %all-reduce.2.cloned.1.call-done = bf16[384,3618]{0,1:T(8,128)(2,1)} async-done(((bf16[384,3618]{0,1:T(8,128)(2,1)}), bf16[384,3618]{0,1:T(8,128)(2,1)}) %all-reduce.2.cloned.1.call-update) | async-done | bytes 2778640 | tf_op jit(solution)/shard_map/psum | solution.py:518
  686.6 4.1 fusion.251
  690.7 3.2 copy.147
  694.7 1.9 copy.148
  697.5 3.0 copy.150
  (340 shorter events, 51.6 us)
Async XLA Ops:
  7.2 121.5 %all-gather.7.cloned.1.call-start = ((), (), s32[]{:S(2)}) async-start(), calls=%async_computation.11 | async-start | bytes 2949120 | tf_op jit(solution)/shard_map/all_gather | solution.py:441
  7.9 170.1 %all-gather.9.cloned.1.call-start = ((), (), s32[]{:S(2)}) async-start(), calls=%async_computation.12 | async-start | bytes 2949120 | tf_op jit(solution)/shard_map/all_gather | solution.py:442
  113.1 4.4 copy-start.12
  117.6 7.0 copy-start.9
  117.6 7.0 copy-start.38
  117.6 52.3 %all-to-all-start = ((bf16[32,40,1536]{2,1,0:T(8,128)(2,1)}), bf16[32,40,1536]{2,1,0:T(8,128)(2,1)}, u32[]{:S(2)}, u32[]{:S(2)}) async-start(bf16[32,40,1536]{2,1,0:T(8,128)(2,1)} %bitcast.111), calls=%async_computation | async-start | bytes 7864320 | tf_op jit(solution)/shard_map/all_to_all | solution.py:423
  122.4 63.5 %all-gather.11.cloned.1.call-start = ((), (), s32[]{:S(2)}) async-start(), calls=%async_computation.13 | async-start | bytes 2949120 | tf_op jit(solution)/shard_map/all_gather | solution.py:443
  126.7 51.3 %copy-start.51 = (f32[256]{0:T(256)}, f32[256]{0:T(256)S(1)}, u32[]{:S(2)}) copy-start(f32[256]{0:T(256)S(1)} %get-tuple-element.128) | copy-start | bytes 3076
  127.6 50.4 %copy-start.53 = (f32[256]{0:T(256)}, f32[256]{0:T(256)S(1)}, u32[]{:S(2)}) copy-start(f32[256]{0:T(256)S(1)} %get-tuple-element.132) | copy-start | bytes 3076
  128.4 84.0 %copy-start.22 = (f32[256,256]{0,1:T(8,128)}, f32[256,256]{0,1:T(8,128)S(1)}, u32[]{:S(2)}) copy-start(f32[256,256]{0,1:T(8,128)S(1)} %get-tuple-element.137) | copy-start | bytes 786436
  128.5 84.0 %copy-start.55 = (f32[256]{0:T(256)}, f32[256]{0:T(256)S(1)}, u32[]{:S(2)}) copy-start(f32[256]{0:T(256)S(1)} %get-tuple-element.136) | copy-start | bytes 3076
  128.7 84.5 %copy-start.13 = (f32[256,256]{0,1:T(8,128)}, f32[256,256]{0,1:T(8,128)S(1)}, u32[]{:S(2)}) copy-start(f32[256,256]{0,1:T(8,128)S(1)} %get-tuple-element.141) | copy-start | bytes 786436
  128.7 84.5 %copy-start.47 = (f32[256]{0:T(256)}, f32[256]{0:T(256)S(1)}, u32[]{:S(2)}) copy-start(f32[256]{0:T(256)S(1)} %get-tuple-element.140) | copy-start | bytes 3076
  185.9 11.1 %copy-start.80 = (bf16[1,1536,768]{2,1,0:T(8,128)(2,1)S(1)}, bf16[1,1536,768]{2,1,0:T(8,128)(2,1)}, u32[]{:S(2)}) copy-start(bf16[1,1536,768]{2,1,0:T(8,128)(2,1)} %all-gather.7.cloned.1.call-done) | copy-start | bytes 7077892
  196.9 3.4 copy-start.88
  196.9 3.4 copy-start.90
  197.0 3.4 copy-start.82
  205.3 54.8 %all-to-all-start.2 = ((bf16[32,40,1536]{2,1,0:T(8,128)(2,1)}), bf16[32,40,1536]{2,1,0:T(8,128)(2,1)}, u32[]{:S(2)}, u32[]{:S(2)}) async-start(bf16[32,40,1536]{2,1,0:T(8,128)(2,1)} %bitcast.113), calls=%async_computation.2 | async-start | bytes 7864320 | tf_op jit(solution)/shard_map/all_to_all | solution.py:423
  212.5 13.7 %copy-start.3 = (bf16[256,1536]{1,0:T(8,128)(2,1)S(1)}, bf16[256,1536]{1,0:T(8,128)(2,1)}, u32[]{:S(2)}) copy-start(bf16[256,1536]{1,0:T(8,128)(2,1)} %tokens.1) | copy-start | bytes 2359300
  214.9 11.5 %copy-start.4 = (f32[256,1536]{1,0:T(8,128)S(1)}, f32[256,1536]{1,0:T(8,128)}, u32[]{:S(2)}) copy-start(f32[256,1536]{1,0:T(8,128)} %get-tuple-element.25) | copy-start | bytes 4718596
  216.8 9.8 %copy-start.24 = (f32[256,256]{0,1:T(8,128)}, f32[256,256]{0,1:T(8,128)S(1)}, u32[]{:S(2)}) copy-start(f32[256,256]{0,1:T(8,128)S(1)} %get-tuple-element.149) | copy-start | bytes 786436
  216.8 9.8 %copy-start.62 = (f32[256]{0:T(256)}, f32[256]{0:T(256)S(1)}, u32[]{:S(2)}) copy-start(f32[256]{0:T(256)S(1)} %get-tuple-element.148) | copy-start | bytes 3076
  218.5 8.1 %copy-start.26 = (f32[256,256]{0,1:T(8,128)}, f32[256,256]{0,1:T(8,128)S(1)}, u32[]{:S(2)}) copy-start(f32[256,256]{0,1:T(8,128)S(1)} %get-tuple-element.153) | copy-start | bytes 786436
  218.5 8.1 %copy-start.64 = (f32[256]{0:T(256)}, f32[256]{0:T(256)S(1)}, u32[]{:S(2)}) copy-start(f32[256]{0:T(256)S(1)} %get-tuple-element.152) | copy-start | bytes 3076
  218.5 8.7 %copy-start.81 = (bf16[1,1536,768]{2,1,0:T(8,128)(2,1)S(1)}, bf16[1,1536,768]{2,1,0:T(8,128)(2,1)}, u32[]{:S(2)}) copy-start(bf16[1,1536,768]{2,1,0:T(8,128)(2,1)} %all-gather.11.cloned.1.call-done) | copy-start | bytes 7077892
  218.5 8.7 %copy-start.89 = (bf16[1280,768]{1,0:T(8,128)(2,1)S(1)}, bf16[1280,768]{1,0:T(8,128)(2,1)}, u32[]{:S(2)}) copy-start(bf16[1280,768]{1,0:T(8,128)(2,1)} %get-tuple-element.84) | copy-start | bytes 5898244
  220.7 11.4 %copy-start.28 = (f32[256,256]{0,1:T(8,128)}, f32[256,256]{0,1:T(8,128)S(1)}, u32[]{:S(2)}) copy-start(f32[256,256]{0,1:T(8,128)S(1)} %get-tuple-element.157) | copy-start | bytes 786436
  220.7 11.4 %copy-start.66 = (f32[256]{0:T(256)}, f32[256]{0:T(256)S(1)}, u32[]{:S(2)}) copy-start(f32[256]{0:T(256)S(1)} %get-tuple-element.156) | copy-start | bytes 3076
  222.4 9.6 %copy-start.68 = (f32[256]{0:T(256)}, f32[256]{0:T(256)S(1)}, u32[]{:S(2)}) copy-start(f32[256]{0:T(256)S(1)} %get-tuple-element.160) | copy-start | bytes 3076
  224.9 7.2 %copy-start.70 = (f32[256]{0:T(256)}, f32[256]{0:T(256)S(1)}, u32[]{:S(2)}) copy-start(f32[256]{0:T(256)S(1)} %get-tuple-element.164) | copy-start | bytes 3076
  260.2 8.1 %copy-start.42 = (f32[32,256]{1,0:T(8,128)S(1)}, f32[32,256]{1,0:T(8,128)}, u32[]{:S(2)}) copy-start(f32[32,256]{1,0:T(8,128)} %get-tuple-element.26) | copy-start | bytes 98308
  260.2 55.6 %all-to-all-start.1 = ((bf16[32,40,1536]{2,1,0:T(8,128)(2,1)}), bf16[32,40,1536]{2,1,0:T(8,128)(2,1)}, u32[]{:S(2)}, u32[]{:S(2)}) async-start(bf16[32,40,1536]{2,1,0:T(8,128)(2,1)} %bitcast.112), calls=%async_computation.1 | async-start | bytes 7864320 | tf_op jit(solution)/shard_map/all_to_all | solution.py:423
  268.1 4.5 copy-start.8
  268.1 203.0 %reduce-scatter.13.cloned.1.call-start = ((), (), s32[]{:S(2)}) async-start(), calls=%async_computation.14 | async-start | bytes 14254080
  268.3 4.3 copy-start.5
  273.1 3.8 copy-start.35
  276.9 5.9 copy-start.84
  276.9 2.9 copy-start.37
  319.2 6.7 copy-start.18
  319.3 6.6 copy-start.52
  319.4 6.6 copy-start.58
  319.4 6.6 copy-start.85
  367.6 138.0 %reduce-scatter.7.cloned.1.call-start = ((), (), s32[]{:S(2)}) async-start(), calls=%async_computation.8 | async-start | bytes 2949120 | tf_op jit(solution)/shard_map/reduce_scatter | solution.py:462
  375.1 165.1 %reduce-scatter.9.cloned.1.call-start = ((), (), s32[]{:S(2)}) async-start(), calls=%async_computation.9 | async-start | bytes 2949120 | tf_op jit(solution)/shard_map/reduce_scatter | solution.py:462
  383.1 191.2 %reduce-scatter.11.cloned.1.call-start = ((), (), s32[]{:S(2)}) async-start(), calls=%async_computation.10 | async-start | bytes 2949120 | tf_op jit(solution)/shard_map/reduce_scatter | solution.py:462
  390.8 295.7 %all-reduce.2.cloned.1.call-start = ((), (), s32[]{:S(2)}) async-start(), calls=%async_computation.7 | async-start | bytes 5566464 | tf_op jit(solution)/shard_map/psum | solution.py:518
  391.8 3.5 copy-start.6
  690.7 3.2 copy-start.2
  (54 other events, 70.1 us)
Sparse Core Ops, SparseCore 0:
  9.7 55.3 all-gather.6
  66.7 44.0 all-gather.8
  124.9 32.2 all-gather.10
  367.7 103.3 reduce-scatter.12
  474.1 31.4 reduce-scatter.6
  508.6 31.5 reduce-scatter.8
  542.7 31.5 reduce-scatter.10
  578.0 108.4 all-reduce.1

commit v2 on v1

--- a/solution.py
+++ b/solution.py
@@ -270,12 +270,12 @@
         dy_out[pl.ds(i * 4, 4)] = (picked * gain).reshape(4, CAP, MODEL_WIDTH).astype(BF16)
 
     sends = [
-        remote(dy_out.at[t], dy_in.at[p.e], as_.at[k], ar.at[k], (p.x, t))
+        remote(dy_out.at[t], dy_in.at[k], as_.at[k], ar.at[k], (p.x, t))
         for k, t in enumerate(peers)
     ]
     for c in sends:
         c.start()
-    own_dy = pltpu.make_async_copy(dy_out.at[p.e], dy_in.at[p.e], ls.at[3])
+    own_dy = pltpu.make_async_copy(dy_out.at[p.e], dy_in.at[31], ls.at[3])
     own_dy.start()
 
     def part(x_index):
@@ -419,6 +419,309 @@
     return value, slope
 
 
+class GatherOwn:
+    def __init__(self, place, shard, region, send, recv):
+        p = place
+
+        def move(k, src, dst, device):
+            return remote(src, dst, send.at[k], recv.at[k], device)
+
+        self.direct = [
+            move(0, shard, region(p.x, 0, SHARD), p.right),
+            move(1, shard, region(p.x, 0, SHARD), p.left),
+        ]
+        from_left = region(p.xl, 0, HALF)
+        from_right = region(p.xr, HALF, HALF)
+        self.forward = [
+            move(2, from_left, from_left, p.right),
+            move(3, from_right, from_right, p.left),
+        ]
+
+    def start(self):
+        for c in self.direct:
+            c.start()
+
+    def relay(self):
+        for k in range(2):
+            self.direct[k].wait_recv()
+            self.forward[k].start()
+
+    def arrived(self):
+        for c in self.forward:
+            c.wait_recv()
+
+    def finish(self):
+        for c in self.direct + self.forward:
+            c.wait_send()
+
+
+class Scatter:
+    def __init__(self, place, partial, landing, send, recv, first=0, height=SHARD):
+        p = self.p = place
+        half = height // 2
+        self.partial, self.landing, self.first, self.height = partial, landing, first, height
+
+        def region(x, part):
+            return partial.at[rows(x * SHARD + first + part * half, half, 32)]
+
+        def move(k, src, device):
+            return remote(src, landing.at[k], send.at[k], recv.at[k], device)
+
+        self.far = [move(0, region(p.x2, 0), p.right), move(1, region(p.x2, 1), p.left)]
+        self.near = [move(2, region(p.xr, 1), p.right), move(3, region(p.xl, 0), p.left)]
+        self.summed = [move(4, region(p.xr, 0), p.right), move(5, region(p.xl, 1), p.left)]
+
+    def relay(self):
+        p, half = self.p, self.height // 2
+        for k, x, part in ((0, p.xr, 0), (1, p.xl, 1)):
+            self.far[k].wait_recv()
+            where = rows(x * SHARD + self.first + part * half, half, 32)
+            self.partial[where, :] = (
+                self.partial[where, :].astype(F32) + self.landing[k].astype(F32)
+            ).astype(BF16)
+            self.summed[k].start()
+
+    def result(self, part, columns=slice(None)):
+        p, half = self.p, self.height // 2
+        own = self.partial[rows(p.x * SHARD + self.first + part * half, half, 32), columns]
+        one, two = ((4, 3), (2, 5))[part]
+        return (
+            own.astype(F32)
+            + self.landing[one, :, columns].astype(F32)
+            + self.landing[two, :, columns].astype(F32)
+        )
+
+    def arrived(self):
+        for c in self.near + self.summed:
+            c.wait_recv()
+
+    def finish(self):
+        for c in self.far + self.near + self.summed:
+            c.wait_send()
+
+
+GROUP = 8
+BLOCK = GROUP * CAP
+
+
+def flatten(slots):
+    return slots.astype(F32).reshape(BLOCK, MODEL_WIDTH).astype(BF16)
+
+
+def unflatten(values):
+    return values.reshape(GROUP, CAP, MODEL_WIDTH).astype(BF16)
+
+
+def expert_kernel(
+    n2, posm, wgate, wup, wdown, dy,
+    dr_in, y_out, g_gate, g_up, g_down,
+    sendbuf, landing, ybuf, rflat, dyflat, wgu, wd, hid, gab, dab, part_down, part_gu, land_down, land_gu,
+    gs, gr, ns, nr, bs, br, ss, sr, ls,
+):
+    p = Place()
+    peers = p.peers()
+    sources = [p.peer(tuple((-v) % m for v, m in zip(o, (4, 4, 2)))) for o in OFFSETS]
+    barrier = greet([p.left, p.right] + [(p.x, t) for t in peers])
+    load_dy = pltpu.make_async_copy(dy, ybuf, ls.at[0])
+    load_dy.start()
+
+    def columns(full, first):
+        return lambda x, start, count: full.at[
+            rows(x * SHARD + start, count, 32), pl.ds(first, FF)
+        ]
+
+    mine = [
+        pltpu.make_async_copy(w, f(p.x, 0, SHARD), ls.at[1 + k])
+        for k, (w, f) in enumerate(
+            [(wgate, columns(wgu, 0)), (wup, columns(wgu, FF)), (wdown, columns(wd, 0))]
+        )
+    ]
+    for c in mine:
+        c.start()
+
+    @pl.loop(0, EXPERTS // 4)
+    def _(i):
+        hot = jnp.concatenate(slot_rows(posm, i * 4, 4), axis=0).astype(BF16)
+        sendbuf[pl.ds(i * 4, 4)] = mm(hot, n2[...]).reshape(4, CAP, MODEL_WIDTH).astype(BF16)
+
+    pl.semaphore_wait(barrier, len(peers) + 2)
+    ggate = GatherOwn(p, wgate, columns(wgu, 0), gs.at[0], gr.at[0])
+    gup = GatherOwn(p, wup, columns(wgu, FF), gs.at[1], gr.at[1])
+    gdown = GatherOwn(p, wdown, columns(wd, 0), gs.at[2], gr.at[2])
+    ggate.start()
+    gup.start()
+    sends = [
+        remote(sendbuf.at[t], landing.at[k], ns.at[k], nr.at[k], (p.x, t))
+        for k, t in enumerate(peers)
+    ]
+    for c in sends:
+        c.start()
+    own_rows = pltpu.make_async_copy(sendbuf.at[p.e], landing.at[31], ls.at[4])
+    own_rows.start()
+
+    load_dy.wait()
+
+    @pl.loop(0, 4)
+    def _(i):
+        dyflat[rows(i * BLOCK, BLOCK), :] = flatten(ybuf[pl.ds(i * GROUP, GROUP)])
+
+    ggate.relay()
+    gup.relay()
+    gdown.start()
+    for c in mine:
+        c.wait()
+    ggate.arrived()
+    gup.arrived()
+
+    for i in range(4):
+        for c in sends[i * GROUP : (i + 1) * GROUP]:
+            c.wait_recv()
+        if i == 3:
+            own_rows.wait()
+        cut = slice(i * BLOCK, (i + 1) * BLOCK)
+        rflat[cut, :] = flatten(landing[i * GROUP : (i + 1) * GROUP])
+        ab = mm(rflat[cut, :], wgu[...])
+        value, slope = gelu_parts(ab[:, :FF])
+        b = ab[:, FF:]
+        hid[cut, :] = (value * b).astype(BF16)
+        gab[cut, :FF] = (slope * b).astype(BF16)
+        gab[cut, FF:] = value.astype(BF16)
+
+    sdown = Scatter(p, part_down, land_down, ss.at[0], sr.at[0])
+    sgu = Scatter(p, part_gu, land_gu, ss.at[1], sr.at[1])
+
+    def down_block(x):
+        where = rows(x * SHARD, SHARD, 128)
+        part_down[where, :] = mm(dyflat[:, where], hid[...], 0, 0).astype(BF16)
+
+    down_block(p.x2)
+    for c in sdown.far:
+        c.start()
+    gdown.relay()
+    down_block(p.xr)
+    sdown.near[0].start()
+    down_block(p.xl)
+    sdown.near[1].start()
+    down_block(p.x)
+    gdown.arrived()
+
+    for c in sends:
+        c.wait_send()
+    backs = []
+    for i in range(4):
+        cut = slice(i * BLOCK, (i + 1) * BLOCK)
+        dh = mm(dyflat[cut, :], wd[...])
+        dab[cut, :FF] = (dh * gab[cut, :FF].astype(F32)).astype(BF16)
+        dab[cut, FF:] = (dh * gab[cut, FF:].astype(F32)).astype(BF16)
+        sendbuf[i * GROUP : (i + 1) * GROUP] = unflatten(mm(dab[cut, :], wgu[...], 1, 1))
+        for k in range(i * GROUP, min((i + 1) * GROUP, 31)):
+            c = remote(sendbuf.at[k], dr_in.at[p.e], bs.at[k], br.at[k], (p.x, sources[k]))
+            c.start()
+            backs.append(c)
+        if i == 1:
+            sdown.relay()
+    own_back = pltpu.make_async_copy(sendbuf.at[31], dr_in.at[p.e], ls.at[5])
+    own_back.start()
+
+    def gu_block(x):
+        where = rows(x * SHARD, SHARD, 128)
+        part_gu[where, :] = mm(rflat[:, where], dab[...], 0, 0).astype(BF16)
+
+    gu_block(p.x2)
+    for c in sgu.far:
+        c.start()
+    gu_block(p.xr)
+    sgu.near[0].start()
+    gu_block(p.xl)
+    sgu.near[1].start()
+    gu_block(p.x)
+
+    for i in range(4):
+        cut = slice(i * BLOCK, (i + 1) * BLOCK)
+        ybuf[i * GROUP : (i + 1) * GROUP] = unflatten(mm(hid[cut, :], wd[...], 1, 1))
+    keep_y = pltpu.make_async_copy(ybuf, y_out, ls.at[6])
+    keep_y.start()
+
+    sdown.arrived()
+    for part in range(2):
+        g_down[part * HALF : (part + 1) * HALF, :] = sdown.result(part)
+    sgu.relay()
+    sgu.arrived()
+    for part in range(2):
+        cut = slice(part * HALF, (part + 1) * HALF)
+        g_gate[cut, :] = sgu.result(part, slice(0, FF))
+        g_up[cut, :] = sgu.result(part, slice(FF, 2 * FF))
+
+    for c in backs:
+        c.wait()
+    own_back.wait()
+    keep_y.wait()
+    for g in (ggate, gup, gdown, sdown, sgu):
+        g.finish()
+
+
+def experts(n2, posm, wgate, wup, wdown, dy):
+    D = MODEL_WIDTH
+
+    def arr(shape, dtype=BF16):
+        return jax.ShapeDtypeStruct(shape, dtype)
+
+    vm = pl.BlockSpec(memory_space=VMEM)
+    hb = pl.BlockSpec(memory_space=ANY)
+    sem = pltpu.SemaphoreType.DMA
+    N = EXPERTS * CAP
+    return pl.pallas_call(
+        expert_kernel,
+        out_shape=[
+            arr((EXPERTS, CAP, D)), arr((EXPERTS, CAP, D)),
+            arr((SHARD, FF), F32), arr((SHARD, FF), F32), arr((SHARD, FF), F32),
+        ],
+        in_specs=[vm] * 5 + [hb],
+        out_specs=[hb, hb, vm, vm, vm],
+        scratch_shapes=[
+            VMEM((EXPERTS, CAP, D), BF16),
+            VMEM((EXPERTS, CAP, D), BF16),
+            VMEM((EXPERTS, CAP, D), BF16),
+            VMEM((N, D), BF16),
+            VMEM((N, D), BF16),
+            VMEM((D, 2 * FF), BF16),
+            VMEM((D, FF), BF16),
+            VMEM((N, FF), BF16),
+            VMEM((N, 2 * FF), BF16),
+            VMEM((N, 2 * FF), BF16),
+            VMEM((D, FF), BF16),
+            VMEM((D, 2 * FF), BF16),
+            VMEM((6, HALF, FF), BF16),
+            VMEM((6, HALF, 2 * FF), BF16),
+            sem((3, 4)),
+            sem((3, 4)),
+            sem((31,)),
+            sem((31,)),
+            sem((31,)),
+            sem((31,)),
+            sem((2, 6)),
+            sem((2, 6)),
+            sem((7,)),
+        ],
+        compiler_params=pltpu.CompilerParams(
+            collective_id=1, has_side_effects=True, vmem_limit_bytes=LIMIT
+        ),
+        name="experts",
+    )(n2, posm, wgate, wup, wdown, dy)
+
+
+def y_slots(y):
+    e = lax.axis_index("expert")
+    z, yy, c = e // 8, lax.rem(e // 2, 4), lax.rem(e, 2)
+    order = jnp.array(OFFSETS + [(0, 0, 0)], jnp.int32)
+    source = (
+        lax.rem(z - order[:, 0] + 4, 4) * 8
+        + lax.rem(yy - order[:, 1] + 4, 4) * 2
+        + lax.rem(c - order[:, 2] + 2, 2)
+    )
+    return jnp.zeros_like(y).at[source].set(y)
+
+
 def exchange(v):
     return lax.all_to_all(v, "expert", split_axis=0, concat_axis=0, tiled=True)
 
@@ -438,32 +741,13 @@
     (dy, fq, fkv, fo, small_all, posm, share, n1, q, kv, o, r, n2) = front(
         tokens, cotangent, routes.T, small, w_query, wkv, w_output
     )
-    gate = lax.all_gather(w_gate[0], "dp", axis=0, tiled=True)
-    up = lax.all_gather(w_up[0], "dp", axis=0, tiled=True)
-    down = lax.all_gather(w_down[0], "dp", axis=0, tiled=True)
+    dR, y, g_gate, g_up, g_down = experts(n2, posm, w_gate[0], w_up[0], w_down[0], dy)
     D = (posm[:, None, :] == jnp.arange(CAP, dtype=F32)[None, :, None]).astype(BF16)
     D = D.reshape(EXPERTS * CAP, SEQ)
     N = EXPERTS * CAP
-    R = exchange(mm(D, n2).astype(BF16).reshape(EXPERTS, CAP, MODEL_WIDTH)).reshape(N, MODEL_WIDTH)
-    dy = dy.reshape(N, MODEL_WIDTH)
-    a = mm(R, gate)
-    b = mm(R, up)
-    value, slope = gelu_parts(a)
-    hid = (value * b).astype(BF16)
-    y = mm(hid, down, 1, 1).astype(BF16)
-    y = exchange(y.reshape(EXPERTS, CAP, MODEL_WIDTH)).reshape(N, MODEL_WIDTH)
-    dh = mm(dy, down)
-    da = (dh * b * slope).astype(BF16)
-    db = (dh * value).astype(BF16)
-    dR = (mm(da, gate, 1, 1) + mm(db, up, 1, 1)).astype(BF16)
-    dR = exchange(dR.reshape(EXPERTS, CAP, MODEL_WIDTH)).reshape(N, MODEL_WIDTH)
-
-    def scatter(v):
-        return lax.psum_scatter(v.astype(BF16), "dp", scatter_dimension=0, tiled=True).astype(F32)
-
-    g_gate = scatter(mm(R, da, 0, 0))[None]
-    g_up = scatter(mm(R, db, 0, 0))[None]
-    g_down = scatter(mm(dy, hid, 0, 0))[None]
+    y = exchange(y_slots(y)).reshape(N, MODEL_WIDTH)
+    dR = dR.reshape(N, MODEL_WIDTH)
+    g_gate, g_up, g_down = g_gate[None], g_up[None], g_down[None]
 
     dz = cotangent.astype(F32)
     gain_one = small_all[:, 32].reshape(-1).astype(F32)

time: 719 us -> 595 us (0.83)
  waiting for transfers between devices: 376 us -> 203 us
  Pallas kernels: 98.7 us -> 200 us
  matrix products: 121 us -> 62.6 us
  local copies, waits for them, and re-layouts: 45.3 us -> 67.9 us
  starting transfers between devices: 20.8 us -> 13 us
  other arithmetic: 31.3 us -> 24 us
    pallas_call x0 -> x1, Pallas kernels: none -> 130 us  [experts(): pl.pallas_call(expert_kernel, out_shape=[arr((EXPERTS, CAP, D)), arr((EXP...]
    all_to_all x3 -> x1, waiting for transfers between devices: 101 us -> 0.01 us  [exchange(): return lax.all_to_all(v, 'expert', split_axis=0, concat_axis=0, tiled=True)]
    reduce_scatter x3 -> x0, waiting for transfers between devices: 91.3 us -> none  [scatter(): lax.psum_scatter(v.astype(BF16), 'dp', scatter_dimension=0, tiled=True)]
    dot_general x82 -> x72, matrix products: 121 us -> 62.6 us  [mm(): lax.dot_general(left, right, (((left_dim,), (right_dim,)), ((), ())), pre...]
    unnamed x9 -> x3, waiting for transfers between devices: 73.6 us -> 104 us
    pallas_call x1, Pallas kernels: 98.7 us -> 70.2 us  [front(): pl.pallas_call(front_kernel, out_shape=outs, in_specs=[vm] * 9, out_specs...]
    scatter x0 -> x1, local copies, waits for them, and re-layouts: none -> 11.2 us  [y_slots(): return jnp.zeros_like(y).at[source].set(y)]
    psum x1, waiting for transfers between devices: 110 us -> 99.1 us  [shards(): part = lax.psum(part, 'expert').astype(F32)]
  transfers between devices with their start and end apart: 11 -> 3, of which waited for: 8 -> 2; matrix products, arithmetic and copies ran while one was open for 15% -> 13% of each run, Pallas kernels for 14% -> 0%
where the time goes in v2:
time: 595 us; the launch traced here: 586 us
  waiting for transfers between devices  203 us (34%)
  Pallas kernels  200 us (34%)
  local copies, waits for them, and re-layouts  67.9 us (11%)
  matrix products  62.6 us (11%)
  other arithmetic  24 us (4%)
  between operations  16.1 us (3%)
  starting transfers between devices  13 us (2%)
    pallas_call x1, Pallas kernels, experts(): pl.pallas_call(expert_kernel, out_shape=[arr((EXPERTS, CAP, D)), arr((EXP...  130 us
    unnamed x3, waiting for transfers between devices  104 us
    psum x1, waiting for transfers between devices, shards(): part = lax.psum(part, 'expert').astype(F32)  99.1 us
    pallas_call x1, Pallas kernels, front(): pl.pallas_call(front_kernel, out_shape=outs, in_specs=[vm] * 9, out_specs...  70.2 us
    dot_general x72, matrix products, mm(): lax.dot_general(left, right, (((left_dim,), (right_dim,)), ((), ())), pre...  62.6 us
    unnamed x224, local copies, waits for them, and re-layouts  38.2 us
    all_to_all x1, starting transfers between devices, exchange(): return lax.all_to_all(v, 'expert', split_axis=0, concat_axis=0, tiled=True)  12.7 us
  transfers between devices with their start and end apart: 3, of which 2 were waited for; matrix products, arithmetic and copies ran while one was open for 13% of the time, Pallas kernels for 0%

profile of v2, /device:TPU:1, one launch (start us, length us, event | category | flops | bytes accessed | tf_op | source)
XLA Modules:
  0.0 586.3 jit_solution(10309941212601562320)
XLA Ops:
  8.6 1.8 pad_maximum_fusion.1.wkv
  10.4 1.4 maximum_maximum_fusion.small
  12.6 70.2 %front.1 = (bf16[32,40,1536]{2,1,0:T(8,128)(2,1)}, bf16[1536,1536]{1,0:T(8,128)(2,1)}, bf16[1536,512]{1,0:T(8,128)(2,1)}, bf16[1536,1536]{1,0:T(8,128)(2,1)}, bf...) custom-call(bf16[256,1536]{1,0:T(8,128)(2,1)} %tokens.1, ...), custom_call_target="tpu_custom_call" | custom-call | tf_op jit(solution)/shard_map/front/pallas_call | solution.py:375
  82.8 129.8 %experts.1 = (bf16[32,40,1536]{2,1,0:T(8,128)(2,1)}, bf16[32,40,1536]{2,1,0:T(8,128)(2,1)}, f32[384,768]{1,0:T(8,128)}, f32[384,768]{1,0:T(8,128)}, f32[384,768]{1,0:T(8,128)}) custom-call(bf16[256,1536]{1,0:T(8,128)(2,1)} %get-tuple-element.33.n2, f32[32,256]{1,0:T(8,128)} %get-tuple-element.31.posm, bf16[384,768]{1,0:T(8,128)(2,1)} %bitcast.76, ...), custom_call_target="tpu_custom_call" | custom-call | tf_op jit(solution)/shard_map/experts/pallas_call | solution.py:673
  212.6 2.1 broadcast_in_dim.40
  214.7 11.2 %scatter_fusion = bf16[32,40,1536]{2,1,0:T(8,128)(2,1)} fusion(bf16[32,40,1536]{2,1,0:T(8,128)(2,1)} %broadcast_in_dim.40, s32[32]{0:T(128)S(1)} %fusion.204, bf16[32,40,1536]{2,1,0:T(8,128)(2,1)} %get-tuple-element.35), kind=kCustom, calls=%fused_computation | custom fusion | bytes 11796608 | tf_op jit(solution)/shard_map/scatter | solution.py:722
  225.9 12.7 %all-to-all-start = ((bf16[32,40,1536]{2,1,0:T(8,128)(2,1)}), bf16[32,40,1536]{2,1,0:T(8,128)(2,1)}, u32[]{:S(2)}, u32[]{:S(2)}) async-start(bf16[32,40,1536]{2,1,0:T(8,128)(2,1)} %scatter_fusion), calls=%async_computation | async-start | bytes 7864320 | tf_op jit(solution)/shard_map/all_to_all | solution.py:726
  238.7 0.9 fusion.270
  239.6 0.9 fusion.269
  240.5 0.9 fusion.268
  241.4 0.9 fusion.267
  242.3 0.9 fusion.266
  243.2 0.9 fusion.265
  244.1 0.9 fusion.264
  245.0 1.5 fusion.263
  246.4 1.5 fusion.262
  247.9 1.5 fusion.261
  249.4 1.5 fusion.260
  250.8 0.9 fusion.259
  251.9 0.9 convert_reduce_fusion
  252.8 4.2 multiply_reduce_fusion
  257.5 3.8 convolution_convert_fusion.3
  287.2 0.8 convolution_add_fusion.8
  288.9 1.1 fusion.122
  290.0 1.2 fusion.121
  291.2 1.2 fusion.120
  297.3 3.9 fusion.271
  301.2 2.5 fusion.11
  303.8 2.7 convolution_convert_fusion.2
  306.5 3.6 convolution_convert_fusion.1
  310.1 3.6 convolution_convert_fusion
  313.8 3.5 fusion.3
  318.1 9.7 %pad_maximum_fusion = bf16[1536,3618]{0,1:T(8,128)(2,1)} fusion(bf16[1536,34]{0,1:T(8,128)(2,1)S(1)} %maximum_bitcast_fusion, bf16[1536,1536]{0,1:T(8,128)(2,1)} %convolution_convert_fusion, bf16[1536,512]{0,1:T(8,128)(2,1)} %convolution_convert_fusion.2, bf16[1536,1536]{0,1:T(8,128)(2,1)} %convolution_convert_fusion.1), kind=kLoop, calls=%fused_computation.1 | loop fusion | flops 44457984 | bytes 22228992 | tf_op jit(solution)/shard_map/concatenate | solution.py:800
  327.8 14.8 %copy.188 = bf16[1536,3618]{1,0:T(8,128)(2,1)} copy(bf16[1536,3618]{0,1:T(8,128)(2,1)} %pad_maximum_fusion) | data formatting | bytes 22228992
  343.6 103.6 %reduce-scatter.4.cloned.1.call-done = bf16[384,3618]{1,0:T(8,128)(2,1)} async-done(((bf16[1536,3618]{1,0:T(8,128)(2,1)}), bf16[384,3618]{1,0:T(8,128)(2,1)}) %reduce-scatter.4.cloned.1.call-update) | async-done | bytes 2778640
  447.2 4.4 copy.189
  451.7 3.4 convolution_bitcast_fusion.1
  455.2 1.7 convolution_add_fusion
  456.9 4.2 fusion.2
  461.1 99.1 %all-reduce.2.cloned.1.call-done = bf16[384,3618]{0,1:T(8,128)(2,1)} async-done(((bf16[384,3618]{0,1:T(8,128)(2,1)}), bf16[384,3618]{0,1:T(8,128)(2,1)}) %all-reduce.2.cloned.1.call-update) | async-done | bytes 2778640 | tf_op jit(solution)/shard_map/psum | solution.py:802
  560.2 3.4 fusion.243
  563.6 1.9 copy.148
  565.6 3.2 copy.151
  570.5 1.9 copy.149
  572.4 0.9 copy.150
  574.0 2.4 copy.207
  576.3 1.0 copy.208
  578.0 1.0 copy.209
  (344 shorter events, 38.4 us)
Async XLA Ops:
  225.9 12.7 %copy-start.9 = (bf16[256,512]{1,0:T(8,128)(2,1)S(1)}, bf16[256,512]{1,0:T(8,128)(2,1)}, u32[]{:S(2)}) copy-start(bf16[256,512]{1,0:T(8,128)(2,1)} %get-tuple-element.39) | copy-start | bytes 786436
  225.9 12.8 %copy-start.44 = (bf16[256,1536]{1,0:T(8,128)(2,1)S(1)}, bf16[256,1536]{1,0:T(8,128)(2,1)}, u32[]{:S(2)}) copy-start(bf16[256,1536]{1,0:T(8,128)(2,1)} %get-tuple-element.38) | copy-start | bytes 2359300
  225.9 87.8 %all-to-all-start = ((bf16[32,40,1536]{2,1,0:T(8,128)(2,1)}), bf16[32,40,1536]{2,1,0:T(8,128)(2,1)}, u32[]{:S(2)}, u32[]{:S(2)}) async-start(bf16[32,40,1536]{2,1,0:T(8,128)(2,1)} %scatter_fusion), calls=%async_computation | async-start | bytes 7864320 | tf_op jit(solution)/shard_map/all_to_all | solution.py:726
  238.6 208.6 %reduce-scatter.4.cloned.1.call-start = ((), (), s32[]{:S(2)}) async-start(), calls=%async_computation.3 | async-start | bytes 14254080
  239.6 26.2 %copy-start.70 = (f32[256]{0:T(256)}, f32[256]{0:T(256)S(1)}, u32[]{:S(2)}) copy-start(f32[256]{0:T(256)S(1)} %get-tuple-element.171) | copy-start | bytes 3076
  240.5 26.7 %copy-start.72 = (f32[256]{0:T(256)}, f32[256]{0:T(256)S(1)}, u32[]{:S(2)}) copy-start(f32[256]{0:T(256)S(1)} %get-tuple-element.167) | copy-start | bytes 3076
  241.4 27.2 %copy-start.74 = (f32[256]{0:T(256)}, f32[256]{0:T(256)S(1)}, u32[]{:S(2)}) copy-start(f32[256]{0:T(256)S(1)} %get-tuple-element.163) | copy-start | bytes 3076
  242.3 27.7 %copy-start.76 = (f32[256]{0:T(256)}, f32[256]{0:T(256)S(1)}, u32[]{:S(2)}) copy-start(f32[256]{0:T(256)S(1)} %get-tuple-element.159) | copy-start | bytes 3076
  243.2 28.2 %copy-start.78 = (f32[256]{0:T(256)}, f32[256]{0:T(256)S(1)}, u32[]{:S(2)}) copy-start(f32[256]{0:T(256)S(1)} %get-tuple-element.155) | copy-start | bytes 3076
  243.2 8.5 %copy-start.4 = (f32[256,1536]{1,0:T(8,128)S(1)}, f32[256,1536]{1,0:T(8,128)}, u32[]{:S(2)}) copy-start(f32[256,1536]{1,0:T(8,128)} %get-tuple-element.30) | copy-start | bytes 4718596
  245.0 28.6 %copy-start.80 = (f32[256]{0:T(256)}, f32[256]{0:T(256)S(1)}, u32[]{:S(2)}) copy-start(f32[256]{0:T(256)S(1)} %get-tuple-element.147) | copy-start | bytes 3076
  247.9 4.9 copy-start.46
  252.8 4.2 copy-start.7
  257.5 3.8 copy-start.40
  261.3 25.9 %copy-start.103 = (bf16[256,1536]{1,0:T(8,128)(2,1)}, bf16[256,1536]{1,0:T(8,128)(2,1)S(1)}, u32[]{:S(2)}) copy-start(bf16[256,1536]{1,0:T(8,128)(2,1)S(1)} %convolution_convert_fusion.3) | copy-start | bytes 2359300
  271.2 2.1 copy-start.34
  273.2 2.1 copy-start.36
  273.2 2.1 copy-start.88
  277.3 2.0 copy-start.90
  282.0 3.1 copy-start.19
  286.8 2.1 copy-start
  286.8 2.1 copy-start.1
  288.1 4.4 copy-start.17
  288.1 4.4 copy-start.64
  288.1 4.4 copy-start.65
  288.1 4.5 copy-start.15
  288.1 4.5 copy-start.62
  288.1 4.5 copy-start.63
  288.9 12.3 %copy-start.98 = (f32[256]{0:T(256)}, f32[256]{0:T(256)S(1)}, u32[]{:S(2)}) copy-start(f32[256]{0:T(256)S(1)} %add_rsqrt_fusion) | copy-start | bytes 3076
  290.0 2.8 copy-start.12
  290.0 2.8 copy-start.60
  290.0 2.8 copy-start.61
  294.8 2.4 copy-start.42
  295.1 6.1 %copy-start.68 = (bf16[256,128]{1,0:T(8,128)(2,1)}, bf16[256,128]{1,0:T(8,128)(2,1)S(1)}, u32[]{:S(2)}) copy-start(bf16[256,128]{1,0:T(8,128)(2,1)S(1)} %fusion.33) | copy-start | bytes 196612
  297.0 4.2 copy-start.69
  297.3 3.9 copy-start.102
  301.2 2.6 copy-start.100
  301.2 2.6 copy-start.6
  303.8 2.8 copy-start.43
  306.5 3.6 copy-start.20
  310.1 3.6 copy-start.47
  310.1 3.7 copy-start.8
  313.8 4.0 copy-start.66
  342.7 217.5 %all-reduce.2.cloned.1.call-start = ((), (), s32[]{:S(2)}) async-start(), calls=%async_computation.2 | async-start | bytes 5566464 | tf_op jit(solution)/shard_map/psum | solution.py:802
  451.7 3.5 copy-start.21
  451.7 3.5 copy-start.99
  565.5 3.2 copy-start.2
  573.3 3.0 copy-start.23
  (62 other events, 78.0 us)
Sparse Core Ops, SparseCore 0:
  342.8 104.3 reduce-scatter.3
  451.8 108.3 all-reduce.1
